TPU v7x, 128 devices: a whole 4x4x4 slice. The times are simulated.
128 devices in a mesh: db: 32 (over x, y, core), pb: 4 (over z).
Axes of the slice: x: 4, y: 4, z: 4, core: 2. Of those that a mesh axis runs over, the one named last changes fastest.
Arguments:
- query_maps: bfloat16 [128, 256, 256], P(('db', 'pb')), may hold values from -6 to 6
- database: bfloat16 [4096, 256, 256], P(('db', 'pb')), may hold values from -6 to 6
- shortlist: int32 [128, 128], P(('db', 'pb')), may hold values from 0 to 4095, as said below
- kernel_query: bfloat16 [3, 3], replicated, may hold values from -1.5 to 1.5
- kernel_db: bfloat16 [3, 3], replicated, may hold values from -1.5 to 1.5
Outputs:
- scores: float32 [128, 128], P(('db', 'pb'))
- top_scores: float32 [128, 100], P(('db', 'pb'))
Inputs may be any that keep to these rules, and one draw needn't show every extreme that they name: Within one query the ids are distinct. Among the 128 shortlist entries of the query held by device q (query q), at most 2 lie in any one shard of images (ids s * 32 to (s + 1) * 32 - 1), and some shard holds exactly 2 of them for every device.
All inputs are finite; a program needn't handle non-finite values.
Results may differ from a plain program's by a relative error of at most 0.0003.
Values may be sent and summed in bfloat16 or wider, within the bound.
No kernel may reach another device: no remote copies, remote signals or barrier semaphores. Data moves between devices by JAX's collectives and lax.ppermute only.
A program may use at most 128 MiB of HBM per device.

v0:
```python
import functools

import jax
import jax.numpy as jnp
from jax import lax
from jax.experimental import pallas as pl
from jax.experimental.pallas import tpu as pltpu
from jax.sharding import Mesh, PartitionSpec as P

GRID = 16
CELLS = GRID * GRID
TOPK = 100
CAND = 128
IMAGES = 32
NODES = 64
CUTS = (0, 80, 176, CELLS)
LARGE = 16
SMALL = 8

epsilon = 1e-06
score_scale = 8.0
f32 = jnp.float32
bf16 = jnp.bfloat16

MAIN = ("x", "y", "c", "z")
NODE = ("x", "y", "z")
OPENING = (("z", True), ("x", True), ("zx", True))
LATE = (("y", True), ("z", False), ("x", False))
GROUP = 8
BLOCK = 4
WAVES = ((0,), (1, 2, 4), (3, 5, 6, 7))


def exchange_pairs(axes, near):
    pairs = []
    for x in range(4):
        for y in range(4):
            for c in range(2):
                for z in range(4):
                    at = {"x": x, "y": y, "z": z}
                    to = dict(at)
                    for axis in axes:
                        to[axis] = at[axis] ^ (1 if (c == 0) == near else 3)
                    pairs.append(
                        (((x * 4 + y) * 2 + c) * 4 + z, ((to["x"] * 4 + to["y"]) * 2 + c) * 4 + to["z"])
                    )
    return pairs


PAIRS = {(axes, near): exchange_pairs(axes, near) for axes in ("x", "y", "z", "zx") for near in (True, False)}


def unit(values):
    squares = jnp.sum(values * values, axis=0, keepdims=True)
    return values * lax.rsqrt(squares + epsilon)


def pack_kernel(query_ref, ids_ref, out_ref):
    out_ref[0, 16:, :] = unit(query_ref[0].astype(f32)).T.astype(bf16)
    ids = ids_ref[...]
    high = lax.shift_right_logical(ids, 6).astype(f32)
    low = (ids & 63).astype(f32)
    row = jnp.concatenate([high, low], axis=1)
    first = lax.broadcasted_iota(jnp.int32, (16, 2 * CAND), 0) == 0
    out_ref[0, :16, :] = jnp.where(first, jnp.broadcast_to(row, first.shape), 0.0).astype(bf16)


def pack(query_maps, shortlist):
    return pl.pallas_call(
        pack_kernel,
        out_shape=jax.ShapeDtypeStruct((1, CELLS + 16, CELLS), bf16),
    )(query_maps, shortlist)


def images_kernel(tap_q_ref, tap_d_ref, maps_hbm, unit_ref, conv_q_ref, conv_d_ref, maps_v, sems):
    copies = []
    for block in range(IMAGES // BLOCK):
        here = pl.ds(block * BLOCK, BLOCK)
        copies.append(pltpu.make_async_copy(maps_hbm.at[here], maps_v.at[here], sems.at[block]))
    for copy in copies:
        copy.start()
    near = lax.broadcasted_iota(jnp.int32, (CELLS, CELLS), 0)
    far = lax.broadcasted_iota(jnp.int32, (CELLS, CELLS), 1)
    for tap_ref, out_ref, result, source in (
        (tap_q_ref, conv_q_ref, near, far),
        (tap_d_ref, conv_d_ref, far, near),
    ):
        down = lax.shift_right_logical(source, 4) - lax.shift_right_logical(result, 4)
        right = (source & (GRID - 1)) - (result & (GRID - 1))
        matrix = jnp.zeros((CELLS, CELLS), f32)
        taps = tap_ref[...].astype(f32)
        for i in range(3):
            for j in range(3):
                hit = (down == i - 1) & (right == j - 1)
                matrix = jnp.where(hit, taps[i : i + 1, j : j + 1], matrix)
        out_ref[...] = matrix.astype(bf16)
    for block, copy in enumerate(copies):
        copy.wait()
        for image in range(block * BLOCK, (block + 1) * BLOCK):
            unit_ref[image] = unit(maps_v[image].astype(f32)).astype(bf16)


def prepare_images(database, tap_q, tap_d):
    vmem = pl.BlockSpec(memory_space=pltpu.VMEM)
    square_shape = jax.ShapeDtypeStruct((CELLS, CELLS), bf16)
    return pl.pallas_call(
        images_kernel,
        in_specs=[vmem, vmem, pl.BlockSpec(memory_space=pl.ANY)],
        out_specs=(vmem, vmem, vmem),
        out_shape=(jax.ShapeDtypeStruct(database.shape, bf16), square_shape, square_shape),
        scratch_shapes=[
            pltpu.VMEM(database.shape, bf16),
            pltpu.SemaphoreType.DMA((IMAGES // BLOCK,)),
        ],
        compiler_params=pltpu.CompilerParams(vmem_limit_bytes=12 * 2**20),
        cost_estimate=pl.CostEstimate(flops=2**24, bytes_accessed=20 * 2**20, transcendentals=0),
    )(tap_q, tap_d, database)


def move(array, step):
    return lax.ppermute(array, MAIN, PAIRS[step])


def orders():
    return [(LATE[piece % 3], LATE[(piece + 1) % 3], LATE[(piece + 2) % 3]) for piece in (0, 2, 1)]


def split(held, own):
    pieces = []
    for piece in range(3):
        first = CUTS[piece] + (16 if piece else 0)
        pieces.append(held[:, first : CUTS[piece + 1] + 16])
    came = [move(p, o[0]) for p, o in zip(pieces, orders())]
    *came, own = lax.optimization_barrier((*came, own))
    return [jnp.concatenate(pair, axis=0) for pair in zip(pieces, came)], own


def sources(combo):
    bits = (combo & 1, combo >> 1 & 1, combo >> 2)
    for turn in (0, 2, 1):
        yield bits[(turn + 1) % 3] + 2 * bits[(turn + 2) % 3], bits[turn]


def pair_kernel(wave, names, place_ref, *refs):
    held = len(WAVES[wave]) * GROUP
    spare = 4 * held
    refs, scratch = refs[:-9], refs[-9:]
    query_v, ids_v, table_v, column_v, peak_v, total_v, table_s, pair_s, sems = scratch
    parts, refs = dict(zip(names, refs)), refs[len(names) :]
    earlier = ()
    if wave == 2:
        earlier, refs = refs[:2], refs[2:]
    if wave == 0:
        own_hbm, other_hbm, conv_q_ref, conv_d_ref, out_ref, image_v = refs[:6]
        image_copies = [
            pltpu.make_async_copy(own_hbm, image_v.at[pl.ds(0, IMAGES)], sems.at[2]),
            pltpu.make_async_copy(other_hbm, image_v.at[pl.ds(IMAGES, IMAGES)], sems.at[3]),
        ]
    else:
        image_v, conv_q_ref, conv_d_ref, out_ref = refs[:4]
        image_copies = []
    id_copies, copies = [], []
    for local, combo in enumerate(WAVES[wave]):
        here = pl.ds(GROUP * local, GROUP)
        for piece, (which, half) in enumerate(sources(combo)):
            source = parts[piece, which]
            blocks = pl.ds(GROUP * half, GROUP)
            size = CUTS[piece + 1] - CUTS[piece]
            skip = 0 if piece else 16
            copies.append(
                pltpu.make_async_copy(
                    source.at[blocks, pl.ds(skip, size), :],
                    query_v.at[here, pl.ds(CUTS[piece], size), :],
                    sems.at[1],
                )
            )
            if piece == 0:
                id_copies.append(
                    pltpu.make_async_copy(
                        source.at[blocks, pl.ds(0, 16), :], ids_v.at[here], sems.at[0]
                    )
                )
    for copy in id_copies + image_copies + copies:
        copy.start()
    pltpu.make_async_copy(ids_v, ids_v, sems.at[0]).wait()
    packed = jnp.sum(ids_v[...].astype(f32), axis=1)
    ids = packed[:, :CAND].astype(jnp.int32) * 64 + packed[:, CAND:].astype(jnp.int32)
    lane = lax.broadcasted_iota(jnp.int32, (held, CAND), 1)
    shard = lax.shift_right_logical(ids, 5)
    slot = ids & (IMAGES - 1)
    table = jnp.full((held, CAND), -1, jnp.int32)
    for side in range(2):
        mine = shard == place_ref[side]
        first = jnp.min(jnp.where(mine, lane, CAND), axis=1, keepdims=True)
        last = jnp.max(jnp.where(mine, lane, -1), axis=1, keepdims=True)
        last = jnp.where(last > first, last, -1)
        for which, column in ((2 * side, first), (2 * side + 1, last)):
            at = lane == column
            image = jnp.max(jnp.where(at, slot, -1), axis=1, keepdims=True)
            image = jnp.where(image >= 0, image + side * IMAGES, -1)
            table = jnp.where(lane == which, image, table)
            column_v[which] = jnp.broadcast_to(column, (held, CAND))
    table_v[...] = table
    move = pltpu.make_async_copy(table_v, table_s, sems.at[4])
    move.start()
    move.wait()

    def fill(query, count):
        for which in range(4):
            image = table_s[query, which]
            pair_s[count] = query * 65536 + (which * held + query) * 64 + jnp.maximum(image, 0)
            count = count + (image >= 0).astype(jnp.int32)
        return count

    count = lax.fori_loop(0, held, fill, jnp.int32(0))
    for extra in range(LARGE):
        pair_s[count + extra] = spare * 64
    for copy in image_copies:
        copy.wait()
    pltpu.make_async_copy(query_v, query_v, sems.at[1]).wait()

    def group(size, base, step, carry):
        found = []
        for part in range(size):
            code = pair_s[base + step * size + part]
            node = lax.shift_right_logical(code, 16)
            image = code & 63
            correlation = jnp.dot(query_v[node], image_v[image], preferred_element_type=f32)
            rectified = jnp.maximum(correlation, 0.0).astype(bf16)
            found.append((lax.shift_right_logical(code, 6) & 1023, rectified))
        for row, rectified in found:
            filtered = jnp.dot(conv_q_ref[...], rectified, preferred_element_type=f32)
            filtered = filtered + jnp.dot(rectified, conv_d_ref[...], preferred_element_type=f32)
            peak_v[pl.ds(row, 1), :] = jnp.max(filtered, axis=0, keepdims=True)
        return carry

    large = (count + LARGE - SMALL - 1) // LARGE
    rest = jnp.maximum(count - large * LARGE, 0)
    lax.fori_loop(0, large, functools.partial(group, LARGE, 0), 0)
    lax.fori_loop(0, (rest + SMALL - 1) // SMALL, functools.partial(group, SMALL, large * LARGE), 0)
    total = jnp.zeros((held, CAND), f32)
    for which in range(4):
        peaks = peak_v[pl.ds(which * held, held), :]
        score = jnp.sum(peaks, axis=1, keepdims=True) * (score_scale / CELLS)
        total = jnp.where(lane == column_v[which], score, total)
    if wave < 2:
        out_ref[...] = total
        return
    done = 0
    for ref in earlier:
        total_v[pl.ds(done, ref.shape[0]), :] = ref[...]
        done += ref.shape[0]
    total_v[pl.ds(done, held), :] = total

    def settle(query, carry):
        out_ref[pl.ds(place_ref[2 + query], 1), :] = total_v[pl.ds(query, 1), :]
        return carry

    lax.fori_loop(0, NODES, settle, 0, unroll=8)


def pair_scores(wave, place, parts, earlier, images, conv_q, conv_d):
    smem = pl.BlockSpec(memory_space=pltpu.SMEM)
    vmem = pl.BlockSpec(memory_space=pltpu.VMEM)
    hbm = pl.BlockSpec(memory_space=pl.ANY)
    held = len(WAVES[wave]) * GROUP
    names = sorted(
        {(piece, which) for combo in WAVES[wave] for piece, (which, _) in enumerate(sources(combo))}
    )
    out_shape = jax.ShapeDtypeStruct((NODES if wave == 2 else held, CAND), f32)
    out_specs = vmem
    image_specs = [vmem]
    if wave == 0:
        out_shape = (out_shape, jax.ShapeDtypeStruct((2 * IMAGES, CELLS, CELLS), bf16))
        out_specs = (vmem, vmem)
        image_specs = [pl.BlockSpec(memory_space=pltpu.HBM)] * 2
    return pl.pallas_call(
        functools.partial(pair_kernel, wave, names),
        out_shape=out_shape,
        in_specs=[smem] + [hbm] * len(names) + [vmem] * len(earlier) + image_specs + [vmem, vmem],
        out_specs=out_specs,
        scratch_shapes=[
            pltpu.VMEM((held, CELLS, CELLS), bf16),
            pltpu.VMEM((held, 16, CELLS), bf16),
            pltpu.VMEM((held, CAND), jnp.int32),
            pltpu.VMEM((4, held, CAND), jnp.int32),
            pltpu.VMEM((4 * held + 8, CELLS), f32),
            pltpu.VMEM((NODES, CAND), f32),
            pltpu.SMEM((held, CAND), jnp.int32),
            pltpu.SMEM((4 * held + LARGE,), jnp.int32),
            pltpu.SemaphoreType.DMA((5,)),
        ],
        compiler_params=pltpu.CompilerParams(vmem_limit_bytes=12 * 2**20),
        cost_estimate=pl.CostEstimate(
            flops=3 * held * 6 * CELLS**3, bytes_accessed=16 * 2**20, transcendentals=0
        ),
    )(place, *[parts[piece][which] for piece, which in names], *earlier, *images, conv_q, conv_d)


def finish_kernel(parts_ref, scores_ref, top_ref):
    row = jnp.sum(parts_ref[...], axis=0, keepdims=True)
    scores_ref[...] = row
    across = jnp.broadcast_to(row, (CAND, CAND))
    down = across.T
    at_row = lax.broadcasted_iota(jnp.int32, (CAND, CAND), 0)
    at_col = lax.broadcasted_iota(jnp.int32, (CAND, CAND), 1)
    ahead = (across > down) | ((across == down) & (at_col < at_row))
    rank = jnp.sum(ahead.astype(f32), axis=1, keepdims=True)
    placed = jnp.where(rank == at_col.astype(f32), down, 0.0)
    top_ref[...] = jnp.sum(placed, axis=0, keepdims=True)[:, :TOPK]


def finish(parts):
    return pl.pallas_call(
        finish_kernel,
        out_shape=(
            jax.ShapeDtypeStruct((1, CAND), f32),
            jax.ShapeDtypeStruct((1, TOPK), f32),
        ),
    )(parts)


def place_table():
    me = lax.axis_index("c")
    x, y, z = [lax.axis_index(axis) for axis in NODE]
    base = (x * 4 + y) * 8 + z
    near = jnp.where(me == 0, 1, 3)
    far = 4 - near
    combos = jnp.array([combo for wave in WAVES for combo in wave], jnp.int32)
    index = (combos[:, None] * GROUP + jnp.arange(GROUP, dtype=jnp.int32)).reshape(-1)
    bit = [lax.shift_right_logical(index, k) & 1 for k in range(6)]
    z = z ^ (bit[0] * near) ^ (bit[4] * far)
    x = x ^ (bit[1] * near) ^ (bit[5] * far)
    y = y ^ (bit[2] * far) ^ (bit[3] * near)
    shards = jnp.stack([base + 4 * me, base + 4 * (1 - me)])
    return jnp.concatenate([shards, (x * 4 + y) * 4 + z]).astype(jnp.int32)


def body(query_maps, database, shortlist, kernel_query, kernel_db):
    held = pack(query_maps, shortlist)
    held = jnp.concatenate([held] + [move(held, step) for step in OPENING], axis=0)
    database, held = lax.optimization_barrier((database, held))
    came = move(held, ("y", False))
    own, conv_q, conv_d = prepare_images(database, kernel_query, kernel_db)
    came, own = lax.optimization_barrier((came, own))
    held = jnp.concatenate([held, came], axis=0)
    place = place_table()
    pieces, own = split(held, own)
    other = lax.ppermute(own, "c", [(0, 1), (1, 0)])
    second = [move(p, o[1]) for p, o in zip(pieces, orders())]
    third = [move(p, o[2]) for p, o in zip(pieces, orders())]
    first_scores, images = pair_scores(
        0, place, [[p] for p in pieces], (), (own, other), conv_q, conv_d
    )
    *second, first_scores = lax.optimization_barrier((*second, first_scores))
    fourth = [move(p, o[2]) for p, o in zip(second, orders())]
    parts = [list(part) for part in zip(pieces, second, third, fourth)]
    second_scores = pair_scores(1, place, parts, (), (images,), conv_q, conv_d)
    earlier = (first_scores, second_scores)
    scores = pair_scores(2, place, parts, earlier, (images,), conv_q, conv_d)
    scores = lax.all_to_all(scores, NODE, split_axis=0, concat_axis=0, tiled=True)
    return finish(scores)


def solution(mesh):
    fine = Mesh(mesh.devices.reshape(4, 4, 2, 4), MAIN)
    in_specs = (P(MAIN, None, None), P(MAIN, None, None), P(MAIN, None), P(), P())
    out_specs = (P(MAIN, None), P(MAIN, None))
    return jax.shard_map(body, mesh=fine, in_specs=in_specs, out_specs=out_specs, check_vma=False)
```

profile of v0, /device:TPU:0, one launch (start us, length us, event | category | flops | bytes accessed | tf_op | source)
XLA Modules:
  0.0 104.5 jit_solution(17254247367623791172)
XLA Ops:
  0.6 0.0 copy-start.2
  0.6 0.0 copy-start.1
  0.7 1.7 %shard_map.77 = bf16[1,272,256]{2,1,0:T(8,128)(2,1)} custom-call(bf16[1,256,256]{2,1,0:T(8,128)(2,1)} %query_ref.1, s32[1,128]{1,0:T(1,128)} %ids_ref.1), custom_call_target="tpu_custom_call" | custom-call | tf_op jit(solution)/shard_map/pallas_call | solution.py:69
  2.4 2.0 %collective-permute-start = (bf16[1,272,256]{2,1,0:T(8,128)(2,1)}, bf16[1,272,256]{2,1,0:T(8,128)(2,1)S(1)}, u32[]{:S(2)}, u32[]{:S(2)}) collective-permute-start(bf16[1,272,256]{2,1,0:T(8,128)(2,1)} %shard_map.77), channel_id=1, source_target_pairs={{0,1},{1,0},{2,3},{3,2},{4,7},{5,6},{6,5},{7,4},{8,9},{9,8},{10,11... | collective-permute-start | bytes 417800 | tf_op jit(solution)/shard_map/ppermute | solution.py:121
  4.4 1.5 %collective-permute-start.1 = (bf16[1,272,256]{2,1,0:T(8,128)(2,1)}, bf16[1,272,256]{2,1,0:T(8,128)(2,1)S(1)}, u32[]{:S(2)}, u32[]{:S(2)}) collective-permute-start(bf16[1,272,256]{2,1,0:T(8,128)(2,1)} %shard_map.77), channel_id=1, source_target_pairs={{0,32},{1,33},{2,34},{3,35},{4,100},{5,101},{6,102},{7,103},{8,40}... | collective-permute-start | bytes 417800 | tf_op jit(solution)/shard_map/ppermute | solution.py:121
  5.9 0.0 collective-permute-start.2
  5.9 1.8 %collective-permute-done = bf16[1,272,256]{2,1,0:T(8,128)(2,1)S(1)} collective-permute-done((bf16[1,272,256]{2,1,0:T(8,128)(2,1)}, bf16[1,272,256]{2,1,0:T(8,128)(2,1)S(1)}, u32[]{:S(2)}, u32[]{:S(2)}) %collective-permute-start) | collective-permute-done | bytes 139296 | tf_op jit(solution)/shard_map/ppermute | solution.py:121
  7.6 2.0 %collective-permute-done.1 = bf16[1,272,256]{2,1,0:T(8,128)(2,1)S(1)} collective-permute-done((bf16[1,272,256]{2,1,0:T(8,128)(2,1)}, bf16[1,272,256]{2,1,0:T(8,128)(2,1)S(1)}, u32[]{:S(2)}, u32[]{:S(2)}) %collective-permute-start.1) | collective-permute-done | bytes 139296 | tf_op jit(solution)/shard_map/ppermute | solution.py:121
  9.6 2.4 %collective-permute-done.2 = bf16[1,272,256]{2,1,0:T(8,128)(2,1)S(1)} collective-permute-done((bf16[1,272,256]{2,1,0:T(8,128)(2,1)}, bf16[1,272,256]{2,1,0:T(8,128)(2,1)S(1)}, u32[]{:S(2)}, u32[]{:S(2)}) %collective-permute-start.2) | collective-permute-done | bytes 139296 | tf_op jit(solution)/shard_map/ppermute | solution.py:121
  12.0 1.0 pad_maximum_fusion.3
  13.0 3.1 %collective-permute-start.3 = (bf16[4,272,256]{2,1,0:T(8,128)(2,1)S(1)}, bf16[4,272,256]{2,1,0:T(8,128)(2,1)S(1)}, u32[]{:S(2)}, u32[]{:S(2)}) collective-permute-start(bf16[4,272,256]{2,1,0:T(8,128)(2,1)S(1)} %pad_maximum_fusion.3), channel_id=1, source_target_pairs={{0,24},{1,25},{2,26},{3,27},{4,12},{5,13},{6,14},{7,15},{8,16},{9,... | collective-permute-start | bytes 1671176 | tf_op jit(solution)/shard_map/ppermute | solution.py:121
  16.1 0.0 copy-done.2
  16.1 0.0 copy-done.1
  16.1 0.0 copy-start
  16.1 2.2 %copy-done = bf16[32,256,256]{2,1,0:T(8,128)(2,1)S(1)} copy-done((bf16[32,256,256]{2,1,0:T(8,128)(2,1)S(1)}, bf16[32,256,256]{2,1,0:T(8,128)(2,1)}, u32[]{:S(2)}) %copy-start) | copy-done | bytes 4194328
  18.3 4.0 %shard_map.78 = (bf16[32,256,256]{2,1,0:T(8,128)(2,1)}, bf16[256,256]{1,0:T(8,128)(2,1)S(1)}, bf16[256,256]{1,0:T(8,128)(2,1)S(1)}) custom-call(bf16[3,3]{1,0:T(4,128)(2,1)S(1)} %copy-done.1, bf16[3,3]{1,0:T(4,128)(2,1)S(1)} %copy-done.2, bf16[32,256,256]{2,1,0:T(8,128)(2,1)S(1)} %copy-done), custom_call_target="tpu_custom_call" | custom-call | flops 16777216 | bytes 20971520 | tf_op jit(solution)/shard_map/pallas_call | solution.py:106
  22.4 1.4 %collective-permute-done.3 = bf16[4,272,256]{2,1,0:T(8,128)(2,1)S(1)} collective-permute-done((bf16[4,272,256]{2,1,0:T(8,128)(2,1)S(1)}, bf16[4,272,256]{2,1,0:T(8,128)(2,1)S(1)}, u32[]{:S(2)}, u32[]{:S(2)}) %collective-permute-start.3) | collective-permute-done | bytes 557088 | tf_op jit(solution)/shard_map/ppermute | solution.py:121
  23.9 0.1 fusion
  23.9 0.4 collective-permute-start.4
  24.4 2.1 %collective-permute-start.5 = (bf16[8,96,256]{2,1,0:T(8,128)(2,1)S(1)}, bf16[8,96,256]{2,1,0:T(8,128)(2,1)S(1)}, u32[]{:S(2)}, u32[]{:S(2)}) collective-permute-start(bf16[8,96,256]{2,1,0:T(8,128)(2,1)S(1)} %get-tuple-element.36), channel_id=1, source_target_pairs={{0,96},{1,97},{2,98},{3,99},{4,36},{5,37},{6,38},{7,39},{8,104},{9... | collective-permute-start | bytes 1179656 | tf_op jit(solution)/shard_map/ppermute | solution.py:121
  26.5 3.4 %collective-permute-start.6 = (bf16[8,80,256]{2,1,0:T(8,128)(2,1)S(1)}, bf16[8,80,256]{2,1,0:T(8,128)(2,1)S(1)}, u32[]{:S(2)}, u32[]{:S(2)}) collective-permute-start(bf16[8,80,256]{2,1,0:T(8,128)(2,1)S(1)} %slice.14), channel_id=1, source_target_pairs={{0,3},{1,2},{2,1},{3,0},{4,5},{5,4},{6,7},{7,6},{8,11},{9,10},{10,... | collective-permute-start | bytes 983048 | tf_op jit(solution)/shard_map/ppermute | solution.py:121
  29.9 5.1 %collective-permute-done.6 = bf16[8,80,256]{2,1,0:T(8,128)(2,1)S(1)} collective-permute-done((bf16[8,80,256]{2,1,0:T(8,128)(2,1)S(1)}, bf16[8,80,256]{2,1,0:T(8,128)(2,1)S(1)}, u32[]{:S(2)}, u32[]{:S(2)}) %collective-permute-start.6) | collective-permute-done | bytes 327712 | tf_op jit(solution)/shard_map/ppermute | solution.py:121
  35.0 0.0 collective-permute-done.4
  35.0 0.0 collective-permute-done.5
  35.0 0.1 collective-permute-start.10
  35.1 0.1 pad_maximum_fusion.2.refs_2_.refs_6_
  35.2 1.0 collective-permute-start.9
  36.2 0.1 pad_maximum_fusion.1.refs_1_.refs_3_
  36.3 0.0 copy-start.5
  36.3 0.1 pad_maximum_fusion.refs_0_
  36.3 1.7 %collective-permute-start.8 = (bf16[16,96,256]{2,1,0:T(8,128)(2,1)S(1)}, bf16[16,96,256]{2,1,0:T(8,128)(2,1)S(1)}, u32[]{:S(2)}, u32[]{:S(2)}) collective-permute-start(bf16[16,96,256]{2,1,0:T(8,128)(2,1)S(1)} %pad_maximum_fusion.1.refs_1_.refs_3_), channel_id=1, source_target_pairs={{0,8},{1,9},{2,10},{3,11},{4,28},{5,29},{6,30},{7,31},{8,0},{9,1},... | collective-permute-start | bytes 2359304 | tf_op jit(solution)/shard_map/ppermute | solution.py:121
  38.1 2.8 %collective-permute-start.7 = (bf16[16,96,256]{2,1,0:T(8,128)(2,1)S(1)}, bf16[16,96,256]{2,1,0:T(8,128)(2,1)}, u32[]{:S(2)}, u32[]{:S(2)}) collective-permute-start(bf16[16,96,256]{2,1,0:T(8,128)(2,1)S(1)} %pad_maximum_fusion.refs_0_), channel_id=1, source_target_pairs={{0,3},{1,2},{2,1},{3,0},{4,5},{5,4},{6,7},{7,6},{8,11},{9,10},{10,... | collective-permute-start | bytes 2359304 | tf_op jit(solution)/shard_map/ppermute | solution.py:121
  40.9 0.5 collective-permute-start.13
  41.3 5.7 %collective-permute-done.9.refs_7_.refs_6_ = bf16[16,80,256]{2,1,0:T(8,128)(2,1)S(1)} collective-permute-done((bf16[16,80,256]{2,1,0:T(8,128)(2,1)S(1)}, bf16[16,80,256]{2,1,0:T(8,128)(2,1)S(1)}, u32[]{:S(2)}, u32[]{:S(2)}) %collective-permute-start.9) | collective-permute-done | bytes 655392 | tf_op jit(solution)/shard_map/ppermute | solution.py:121
  47.0 0.0 copy-start.3
  47.0 0.8 copy-done.3
  47.9 0.9 collective-permute-start.11
  48.8 0.0 collective-permute-done.10.refs_4_
  48.8 1.7 %collective-permute-start.15 = (bf16[16,80,256]{2,1,0:T(8,128)(2,1)S(1)}, bf16[16,80,256]{2,1,0:T(8,128)(2,1)}, u32[]{:S(2)}, u32[]{:S(2)}) collective-permute-start(bf16[16,80,256]{2,1,0:T(8,128)(2,1)S(1)} %pad_maximum_fusion.2.refs_2_.refs_6_), channel_id=1, source_target_pairs={{0,8},{1,9},{2,10},{3,11},{4,28},{5,29},{6,30},{7,31},{8,0},{9,1},... | collective-permute-start | bytes 1966088 | tf_op jit(solution)/shard_map/ppermute | solution.py:121
  50.5 0.0 copy-done.5
  50.5 0.1 multiply_add_fusion
  50.6 0.1 reshape.62
  50.7 0.1 pad_add_fusion.place_ref
  50.7 0.0 copy-start.4
  50.7 7.0 %shard_map.79 = (f32[8,128]{1,0:T(8,128)S(1)}, bf16[64,256,256]{2,1,0:T(8,128)(2,1)S(1)}) custom-call(s32[66]{0:T(128)S(1)} %pad_add_fusion.place_ref, bf16[16,96,256]{2,1,0:T(8,128)(2,1)S(1)} %pad_maximum_fusion.refs_0_, bf16[16,96,256]{2,1,0:T(8,128)(2,1)S(1)} %pad_maximum_fusion.1.refs_1_.refs_3_, ...), custom_call_target="tpu_custom_call" | custom-call | flops 2415919104 | bytes 16777216 | tf_op jit(solution)/shard_map/pallas_call | solution.py:277
  57.8 0.0 collective-permute-done.8.refs_4_.refs_3_
  57.8 0.0 collective-permute-done.7.refs_1_.refs_0_
  57.8 1.3 %collective-permute-start.12 = (bf16[16,96,256]{2,1,0:T(8,128)(2,1)}, bf16[16,96,256]{2,1,0:T(8,128)(2,1)S(1)}, u32[]{:S(2)}, u32[]{:S(2)}) collective-permute-start(bf16[16,96,256]{2,1,0:T(8,128)(2,1)} %collective-permute-done.7.refs_1_.refs_0_), channel_id=1, source_target_pairs={{0,96},{1,97},{2,98},{3,99},{4,36},{5,37},{6,38},{7,39},{8,104},{9... | collective-permute-start | bytes 2359304 | tf_op jit(solution)/shard_map/ppermute | solution.py:121
  59.1 4.3 %collective-permute-start.14 = (bf16[16,96,256]{2,1,0:T(8,128)(2,1)S(1)}, bf16[16,96,256]{2,1,0:T(8,128)(2,1)S(1)}, u32[]{:S(2)}, u32[]{:S(2)}) collective-permute-start(bf16[16,96,256]{2,1,0:T(8,128)(2,1)S(1)} %collective-permute-done.8.refs_4_.refs_3_), channel_id=1, source_target_pairs={{0,3},{1,2},{2,1},{3,0},{4,5},{5,4},{6,7},{7,6},{8,11},{9,10},{10,... | collective-permute-start | bytes 2359304 | tf_op jit(solution)/shard_map/ppermute | solution.py:121
  63.3 0.0 collective-permute-done.15.refs_8_.refs_7_
  63.3 0.0 copy-done.4
  63.3 0.4 collective-permute-start.16
  63.7 0.0 collective-permute-done.13.refs_5_.refs_4_
  63.7 0.0 collective-permute-done.11.refs_2_.refs_1_
  63.7 9.9 %shard_map.80.refs_10_ = f32[24,128]{1,0:T(8,128)S(1)} custom-call(s32[66]{0:T(128)S(1)} %pad_add_fusion.place_ref, bf16[16,96,256]{2,1,0:T(8,128)(2,1)S(1)} %pad_maximum_fusion.refs_0_, bf16[16,96,256]{2,1,0:T(8,128)(2,1)} %collective-permute-done.7.refs_1_.refs_0_, bf16[16,96,256]{2,1,0:T(8,128)(2,1)} %collective-permute-done.11.refs_2_.refs_1_, ...), custom_call_target="tpu_custom_call" | custom-call | flops 7247757312 | bytes 16777216 | tf_op jit(solution)/shard_map/pallas_call | solution.py:277
  73.6 0.3 collective-permute-done.16.refs_8_
  73.9 0.0 collective-permute-done.12.refs_2_
  73.9 0.0 collective-permute-done.14.refs_5_
  73.9 10.9 %shard_map.81 = f32[64,128]{1,0:T(8,128)S(1)} custom-call(s32[66]{0:T(128)S(1)} %pad_add_fusion.place_ref, bf16[16,96,256]{2,1,0:T(8,128)(2,1)} %collective-permute-done.7.refs_1_.refs_0_, bf16[16,96,256]{2,1,0:T(8,128)(2,1)} %collective-permute-done.11.refs_2_.refs_1_, bf16[16,96,256]{2,1,0:T(8,128)(2,1)S(1)} %collective-permute-done.12.refs_2_, ...), custom_call_target="tpu_custom_call" | custom-call | flops 9663676416 | bytes 16777216 | tf_op jit(solution)/shard_map/pallas_call | solution.py:277
  84.8 18.2 %all_to_all.11 = f32[64,1,128]{2,1,0:T(1,128)} all-to-all(f32[64,1,128]{2,1,0:T(1,128)S(1)} %bitcast.6), channel_id=1, replica_groups=mesh['x'=4,'y'=4,'c'=2,'z'=4] {'x','y','z'}, dimensions={0} | all-to-all | bytes 65536 | tf_op jit(solution)/shard_map/all_to_all | solution.py:361
  103.0 1.5 %shard_map.82 = (f32[1,128]{1,0:T(1,128)}, f32[1,100]{1,0:T(1,128)}) custom-call(f32[64,128]{1,0:T(8,128)} %bitcast.7), custom_call_target="tpu_custom_call" | custom-call | tf_op jit(solution)/shard_map/pallas_call | solution.py:314
  (3 shorter events, 0.1 us)
Async XLA Ops:
  0.6 15.5 %copy-start.2 = (bf16[3,3]{1,0:T(4,128)(2,1)S(1)}, bf16[3,3]{1,0:T(4,128)(2,1)}, u32[]{:S(2)}) copy-start(bf16[3,3]{1,0:T(4,128)(2,1)} %tap_d_ref.1) | copy-start | bytes 58
  0.6 15.5 %copy-start.1 = (bf16[3,3]{1,0:T(4,128)(2,1)S(1)}, bf16[3,3]{1,0:T(4,128)(2,1)}, u32[]{:S(2)}) copy-start(bf16[3,3]{1,0:T(4,128)(2,1)} %tap_q_ref.1) | copy-start | bytes 58
  2.4 5.3 %collective-permute-start = (bf16[1,272,256]{2,1,0:T(8,128)(2,1)}, bf16[1,272,256]{2,1,0:T(8,128)(2,1)S(1)}, u32[]{:S(2)}, u32[]{:S(2)}) collective-permute-start(bf16[1,272,256]{2,1,0:T(8,128)(2,1)} %shard_map.77), channel_id=1, source_target_pairs={{0,1},{1,0},{2,3},{3,2},{4,7},{5,6},{6,5},{7,4},{8,9},{9,8},{10,11... | collective-permute-start | bytes 417800 | tf_op jit(solution)/shard_map/ppermute | solution.py:121
  4.4 5.3 %collective-permute-start.1 = (bf16[1,272,256]{2,1,0:T(8,128)(2,1)}, bf16[1,272,256]{2,1,0:T(8,128)(2,1)S(1)}, u32[]{:S(2)}, u32[]{:S(2)}) collective-permute-start(bf16[1,272,256]{2,1,0:T(8,128)(2,1)} %shard_map.77), channel_id=1, source_target_pairs={{0,32},{1,33},{2,34},{3,35},{4,100},{5,101},{6,102},{7,103},{8,40}... | collective-permute-start | bytes 417800 | tf_op jit(solution)/shard_map/ppermute | solution.py:121
  5.9 6.2 %collective-permute-start.2 = (bf16[1,272,256]{2,1,0:T(8,128)(2,1)}, bf16[1,272,256]{2,1,0:T(8,128)(2,1)S(1)}, u32[]{:S(2)}, u32[]{:S(2)}) collective-permute-start(bf16[1,272,256]{2,1,0:T(8,128)(2,1)} %shard_map.77), channel_id=1, source_target_pairs={{0,33},{1,32},{2,35},{3,34},{4,103},{5,102},{6,101},{7,100},{8,41}... | collective-permute-start | bytes 417800 | tf_op jit(solution)/shard_map/ppermute | solution.py:121
  13.0 10.8 %collective-permute-start.3 = (bf16[4,272,256]{2,1,0:T(8,128)(2,1)S(1)}, bf16[4,272,256]{2,1,0:T(8,128)(2,1)S(1)}, u32[]{:S(2)}, u32[]{:S(2)}) collective-permute-start(bf16[4,272,256]{2,1,0:T(8,128)(2,1)S(1)} %pad_maximum_fusion.3), channel_id=1, source_target_pairs={{0,24},{1,25},{2,26},{3,27},{4,12},{5,13},{6,14},{7,15},{8,16},{9,... | collective-permute-start | bytes 1671176 | tf_op jit(solution)/shard_map/ppermute | solution.py:121
  16.1 2.2 %copy-start = (bf16[32,256,256]{2,1,0:T(8,128)(2,1)S(1)}, bf16[32,256,256]{2,1,0:T(8,128)(2,1)}, u32[]{:S(2)}) copy-start(bf16[32,256,256]{2,1,0:T(8,128)(2,1)} %maps_hbm) | copy-start | bytes 12582916
  23.9 11.1 %collective-permute-start.4 = (bf16[8,96,256]{2,1,0:T(8,128)(2,1)S(1)}, bf16[8,96,256]{2,1,0:T(8,128)(2,1)S(1)}, u32[]{:S(2)}, u32[]{:S(2)}) collective-permute-start(bf16[8,96,256]{2,1,0:T(8,128)(2,1)S(1)} %get-tuple-element.37), channel_id=1, source_target_pairs={{0,8},{1,9},{2,10},{3,11},{4,28},{5,29},{6,30},{7,31},{8,0},{9,1},... | collective-permute-start | bytes 1179656 | tf_op jit(solution)/shard_map/ppermute | solution.py:121
  24.4 10.6 %collective-permute-start.5 = (bf16[8,96,256]{2,1,0:T(8,128)(2,1)S(1)}, bf16[8,96,256]{2,1,0:T(8,128)(2,1)S(1)}, u32[]{:S(2)}, u32[]{:S(2)}) collective-permute-start(bf16[8,96,256]{2,1,0:T(8,128)(2,1)S(1)} %get-tuple-element.36), channel_id=1, source_target_pairs={{0,96},{1,97},{2,98},{3,99},{4,36},{5,37},{6,38},{7,39},{8,104},{9... | collective-permute-start | bytes 1179656 | tf_op jit(solution)/shard_map/ppermute | solution.py:121
  26.5 8.5 %collective-permute-start.6 = (bf16[8,80,256]{2,1,0:T(8,128)(2,1)S(1)}, bf16[8,80,256]{2,1,0:T(8,128)(2,1)S(1)}, u32[]{:S(2)}, u32[]{:S(2)}) collective-permute-start(bf16[8,80,256]{2,1,0:T(8,128)(2,1)S(1)} %slice.14), channel_id=1, source_target_pairs={{0,3},{1,2},{2,1},{3,0},{4,5},{5,4},{6,7},{7,6},{8,11},{9,10},{10,... | collective-permute-start | bytes 983048 | tf_op jit(solution)/shard_map/ppermute | solution.py:121
  35.0 13.8 %collective-permute-start.10 = (bf16[32,256,256]{2,1,0:T(8,128)(2,1)}, bf16[32,256,256]{2,1,0:T(8,128)(2,1)}, u32[]{:S(2)}, u32[]{:S(2)}) collective-permute-start(bf16[32,256,256]{2,1,0:T(8,128)(2,1)} %get-tuple-element.27.refs_3_), channel_id=1, source_target_pairs={{0,4},{4,0},{1,5},{5,1},{2,6},{6,2},{3,7},{7,3},{8,12},{12,8},{9,1... | collective-permute-start | bytes 12582920 | tf_op jit(solution)/shard_map/ppermute | solution.py:349
  35.2 11.9 %collective-permute-start.9 = (bf16[16,80,256]{2,1,0:T(8,128)(2,1)S(1)}, bf16[16,80,256]{2,1,0:T(8,128)(2,1)S(1)}, u32[]{:S(2)}, u32[]{:S(2)}) collective-permute-start(bf16[16,80,256]{2,1,0:T(8,128)(2,1)S(1)} %pad_maximum_fusion.2.refs_2_.refs_6_), channel_id=1, source_target_pairs={{0,96},{1,97},{2,98},{3,99},{4,36},{5,37},{6,38},{7,39},{8,104},{9... | collective-permute-start | bytes 1966088 | tf_op jit(solution)/shard_map/ppermute | solution.py:121
  36.3 14.2 %copy-start.5 = (s32[8]{0:T(128)S(1)}, s32[8]{0:T(128)}, u32[]{:S(2)}) copy-start(s32[8]{0:T(128)} %constant.41) | copy-start | bytes 100
  36.3 21.4 %collective-permute-start.8 = (bf16[16,96,256]{2,1,0:T(8,128)(2,1)S(1)}, bf16[16,96,256]{2,1,0:T(8,128)(2,1)S(1)}, u32[]{:S(2)}, u32[]{:S(2)}) collective-permute-start(bf16[16,96,256]{2,1,0:T(8,128)(2,1)S(1)} %pad_maximum_fusion.1.refs_1_.refs_3_), channel_id=1, source_target_pairs={{0,8},{1,9},{2,10},{3,11},{4,28},{5,29},{6,30},{7,31},{8,0},{9,1},... | collective-permute-start | bytes 2359304 | tf_op jit(solution)/shard_map/ppermute | solution.py:121
  38.1 19.7 %collective-permute-start.7 = (bf16[16,96,256]{2,1,0:T(8,128)(2,1)S(1)}, bf16[16,96,256]{2,1,0:T(8,128)(2,1)}, u32[]{:S(2)}, u32[]{:S(2)}) collective-permute-start(bf16[16,96,256]{2,1,0:T(8,128)(2,1)S(1)} %pad_maximum_fusion.refs_0_), channel_id=1, source_target_pairs={{0,3},{1,2},{2,1},{3,0},{4,5},{5,4},{6,7},{7,6},{8,11},{9,10},{10,... | collective-permute-start | bytes 2359304 | tf_op jit(solution)/shard_map/ppermute | solution.py:121
  40.9 22.8 %collective-permute-start.13 = (bf16[16,96,256]{2,1,0:T(8,128)(2,1)S(1)}, bf16[16,96,256]{2,1,0:T(8,128)(2,1)}, u32[]{:S(2)}, u32[]{:S(2)}) collective-permute-start(bf16[16,96,256]{2,1,0:T(8,128)(2,1)S(1)} %pad_maximum_fusion.1.refs_1_.refs_3_), channel_id=1, source_target_pairs={{0,3},{1,2},{2,1},{3,0},{4,5},{5,4},{6,7},{7,6},{8,11},{9,10},{10,... | collective-permute-start | bytes 2359304 | tf_op jit(solution)/shard_map/ppermute | solution.py:121
  47.0 0.8 copy-start.3
  47.9 15.8 %collective-permute-start.11 = (bf16[16,96,256]{2,1,0:T(8,128)(2,1)S(1)}, bf16[16,96,256]{2,1,0:T(8,128)(2,1)}, u32[]{:S(2)}, u32[]{:S(2)}) collective-permute-start(bf16[16,96,256]{2,1,0:T(8,128)(2,1)S(1)} %pad_maximum_fusion.refs_0_), channel_id=1, source_target_pairs={{0,96},{1,97},{2,98},{3,99},{4,36},{5,37},{6,38},{7,39},{8,104},{9... | collective-permute-start | bytes 2359304 | tf_op jit(solution)/shard_map/ppermute | solution.py:121
  48.8 14.5 %collective-permute-start.15 = (bf16[16,80,256]{2,1,0:T(8,128)(2,1)S(1)}, bf16[16,80,256]{2,1,0:T(8,128)(2,1)}, u32[]{:S(2)}, u32[]{:S(2)}) collective-permute-start(bf16[16,80,256]{2,1,0:T(8,128)(2,1)S(1)} %pad_maximum_fusion.2.refs_2_.refs_6_), channel_id=1, source_target_pairs={{0,8},{1,9},{2,10},{3,11},{4,28},{5,29},{6,30},{7,31},{8,0},{9,1},... | collective-permute-start | bytes 1966088 | tf_op jit(solution)/shard_map/ppermute | solution.py:121
  50.7 12.6 %copy-start.4 = (bf16[16,80,256]{2,1,0:T(8,128)(2,1)S(1)}, bf16[16,80,256]{2,1,0:T(8,128)(2,1)}, u32[]{:S(2)}) copy-start(bf16[16,80,256]{2,1,0:T(8,128)(2,1)} %copy-done.3) | copy-start | bytes 1966084
  57.8 16.1 %collective-permute-start.12 = (bf16[16,96,256]{2,1,0:T(8,128)(2,1)}, bf16[16,96,256]{2,1,0:T(8,128)(2,1)S(1)}, u32[]{:S(2)}, u32[]{:S(2)}) collective-permute-start(bf16[16,96,256]{2,1,0:T(8,128)(2,1)} %collective-permute-done.7.refs_1_.refs_0_), channel_id=1, source_target_pairs={{0,96},{1,97},{2,98},{3,99},{4,36},{5,37},{6,38},{7,39},{8,104},{9... | collective-permute-start | bytes 2359304 | tf_op jit(solution)/shard_map/ppermute | solution.py:121
  59.1 14.9 %collective-permute-start.14 = (bf16[16,96,256]{2,1,0:T(8,128)(2,1)S(1)}, bf16[16,96,256]{2,1,0:T(8,128)(2,1)S(1)}, u32[]{:S(2)}, u32[]{:S(2)}) collective-permute-start(bf16[16,96,256]{2,1,0:T(8,128)(2,1)S(1)} %collective-permute-done.8.refs_4_.refs_3_), channel_id=1, source_target_pairs={{0,3},{1,2},{2,1},{3,0},{4,5},{5,4},{6,7},{7,6},{8,11},{9,10},{10,... | collective-permute-start | bytes 2359304 | tf_op jit(solution)/shard_map/ppermute | solution.py:121
  63.3 10.6 %collective-permute-start.16 = (bf16[16,80,256]{2,1,0:T(8,128)(2,1)S(1)}, bf16[16,80,256]{2,1,0:T(8,128)(2,1)S(1)}, u32[]{:S(2)}, u32[]{:S(2)}) collective-permute-start(bf16[16,80,256]{2,1,0:T(8,128)(2,1)S(1)} %copy-done.4), channel_id=1, source_target_pairs={{0,8},{1,9},{2,10},{3,11},{4,28},{5,29},{6,30},{7,31},{8,0},{9,1},... | collective-permute-start | bytes 1966088 | tf_op jit(solution)/shard_map/ppermute | solution.py:121
where the time goes:
time: 105 us; the launch traced here: 104 us
  Pallas kernels  35.1 us (33%)
  starting transfers between devices  27.1 us (26%)
  waiting for transfers between devices  18.7 us (18%)
  blocking collectives  18.2 us (17%)
  local copies, waits for them, and re-layouts  3.3 us (3%)
  other arithmetic  1.34 us (1%)
    pallas_call x3, Pallas kernels, pair_scores(): pl.pallas_call(functools.partial(pair_kernel, wave, names), out_shape=out...  27.9 us
    ppermute x16, starting transfers between devices, move(): return lax.ppermute(array, MAIN, PAIRS[step])  27 us
    ppermute x16, waiting for transfers between devices, move(): return lax.ppermute(array, MAIN, PAIRS[step])  18.7 us
    all_to_all x1, blocking collectives, body(): lax.all_to_all(scores, NODE, split_axis=0, concat_axis=0, tiled=True)  18.2 us
    pallas_call x1, Pallas kernels, prepare_images(): pl.pallas_call(images_kernel, in_specs=[vmem, vmem, pl.BlockSpec(memory_s...  4.04 us
    unnamed x13, local copies, waits for them, and re-layouts  3.09 us
  transfers between devices with their start and end apart: 17, of which 7 were waited for; matrix products, arithmetic and copies ran while one was open for 0% of the time, Pallas kernels for 20%

commit v1 on v0

--- a/solution.py
+++ b/solution.py
@@ -24,14 +24,16 @@
 
 MAIN = ("x", "y", "c", "z")
 NODE = ("x", "y", "z")
-OPENING = (("z", True), ("x", True), ("zx", True))
-LATE = (("y", True), ("z", False), ("x", False))
+FIRST = (("z", True), ("x", True), ("y", False))
+OPENING = tuple(tuple(FIRST[k] for k in range(3) if code >> k & 1) for code in range(1, 8))
+LATE = ((("y", True),), (("z", False),), (("x", False),))
+STEPS = OPENING + LATE
 GROUP = 8
 BLOCK = 4
 WAVES = ((0,), (1, 2, 4), (3, 5, 6, 7))
 
 
-def exchange_pairs(axes, near):
+def exchange_pairs(turns):
     pairs = []
     for x in range(4):
         for y in range(4):
@@ -39,7 +41,7 @@
                 for z in range(4):
                     at = {"x": x, "y": y, "z": z}
                     to = dict(at)
-                    for axis in axes:
+                    for axis, near in turns:
                         to[axis] = at[axis] ^ (1 if (c == 0) == near else 3)
                     pairs.append(
                         (((x * 4 + y) * 2 + c) * 4 + z, ((to["x"] * 4 + to["y"]) * 2 + c) * 4 + to["z"])
@@ -47,7 +49,7 @@
     return pairs
 
 
-PAIRS = {(axes, near): exchange_pairs(axes, near) for axes in ("x", "y", "z", "zx") for near in (True, False)}
+PAIRS = {step: exchange_pairs(step) for step in STEPS}
 
 
 def unit(values):
@@ -340,10 +342,7 @@
     held = pack(query_maps, shortlist)
     held = jnp.concatenate([held] + [move(held, step) for step in OPENING], axis=0)
     database, held = lax.optimization_barrier((database, held))
-    came = move(held, ("y", False))
     own, conv_q, conv_d = prepare_images(database, kernel_query, kernel_db)
-    came, own = lax.optimization_barrier((came, own))
-    held = jnp.concatenate([held, came], axis=0)
     place = place_table()
     pieces, own = split(held, own)
     other = lax.ppermute(own, "c", [(0, 1), (1, 0)])

time: 105 us -> 104 us (level)
  starting transfers between devices: 27.1 us -> 31.6 us
  waiting for transfers between devices: 18.7 us -> 15.1 us
  blocking collectives: 18.2 us -> 15.7 us
  Pallas kernels: 35.1 us -> 37 us
  local copies, waits for them, and re-layouts: 3.3 us -> 2.18 us
    ppermute x16 -> x19, starting transfers between devices: 27 us -> 31.6 us  [move(): return lax.ppermute(array, MAIN, PAIRS[step])]
    ppermute x16 -> x19, waiting for transfers between devices: 18.7 us -> 15.1 us  [move(): return lax.ppermute(array, MAIN, PAIRS[step])]
    all_to_all x1, blocking collectives: 18.2 us -> 15.7 us  [body(): lax.all_to_all(scores, NODE, split_axis=0, concat_axis=0, tiled=True)]
    pallas_call x3, Pallas kernels: 27.9 us -> 29.7 us  [pair_scores(): pl.pallas_call(functools.partial(pair_kernel, wave, names), out_shape=out...]
    unnamed x13 -> x19, local copies, waits for them, and re-layouts: 3.09 us -> 2 us
  transfers between devices with their start and end apart: 17 -> 20, of which waited for: 7 -> 5; matrix products, arithmetic and copies ran while one was open for 0% -> 2% of each run, Pallas kernels for 20% -> 21%
where the time goes in v1:
time: 104 us; the launch traced here: 103 us
  Pallas kernels  37 us (36%)
  starting transfers between devices  31.6 us (30%)
  blocking collectives  15.7 us (15%)
  waiting for transfers between devices  15.1 us (15%)
  local copies, waits for them, and re-layouts  2.18 us (2%)
    ppermute x19, starting transfers between devices, move(): return lax.ppermute(array, MAIN, PAIRS[step])  31.6 us
    pallas_call x3, Pallas kernels, pair_scores(): pl.pallas_call(functools.partial(pair_kernel, wave, names), out_shape=out...  29.7 us
    all_to_all x1, blocking collectives, body(): lax.all_to_all(scores, NODE, split_axis=0, concat_axis=0, tiled=True)  15.7 us
    ppermute x19, waiting for transfers between devices, move(): return lax.ppermute(array, MAIN, PAIRS[step])  15.1 us
    pallas_call x1, Pallas kernels, prepare_images(): pl.pallas_call(images_kernel, in_specs=[vmem, vmem, pl.BlockSpec(memory_s...  4.04 us
  transfers between devices with their start and end apart: 20, of which 5 were waited for; matrix products, arithmetic and copies ran while one was open for 2% of the time, Pallas kernels for 21%

profile of v1, /device:TPU:0, one launch (start us, length us, event | category | flops | bytes accessed | tf_op | source)
XLA Modules:
  0.0 102.8 jit_solution(7780551038949440177)
XLA Ops:
  0.6 1.7 %shard_map.77 = bf16[1,272,256]{2,1,0:T(8,128)(2,1)} custom-call(bf16[1,256,256]{2,1,0:T(8,128)(2,1)} %query_ref.1, s32[1,128]{1,0:T(1,128)} %ids_ref.1), custom_call_target="tpu_custom_call" | custom-call | tf_op jit(solution)/shard_map/pallas_call | solution.py:71
  2.3 2.0 %collective-permute-start = (bf16[1,272,256]{2,1,0:T(8,128)(2,1)}, bf16[1,272,256]{2,1,0:T(8,128)(2,1)S(1)}, u32[]{:S(2)}, u32[]{:S(2)}) collective-permute-start(bf16[1,272,256]{2,1,0:T(8,128)(2,1)} %shard_map.77), channel_id=1, source_target_pairs={{0,1},{1,0},{2,3},{3,2},{4,7},{5,6},{6,5},{7,4},{8,9},{9,8},{10,11... | collective-permute-start | bytes 417800 | tf_op jit(solution)/shard_map/ppermute | solution.py:123
  4.3 1.5 %collective-permute-start.1 = (bf16[1,272,256]{2,1,0:T(8,128)(2,1)}, bf16[1,272,256]{2,1,0:T(8,128)(2,1)S(1)}, u32[]{:S(2)}, u32[]{:S(2)}) collective-permute-start(bf16[1,272,256]{2,1,0:T(8,128)(2,1)} %shard_map.77), channel_id=1, source_target_pairs={{0,32},{1,33},{2,34},{3,35},{4,100},{5,101},{6,102},{7,103},{8,40}... | collective-permute-start | bytes 417800 | tf_op jit(solution)/shard_map/ppermute | solution.py:123
  5.8 0.0 collective-permute-start.2
  5.8 3.1 %collective-permute-start.3 = (bf16[1,272,256]{2,1,0:T(8,128)(2,1)}, bf16[1,272,256]{2,1,0:T(8,128)(2,1)S(1)}, u32[]{:S(2)}, u32[]{:S(2)}) collective-permute-start(bf16[1,272,256]{2,1,0:T(8,128)(2,1)} %shard_map.77), channel_id=1, source_target_pairs={{0,24},{1,25},{2,26},{3,27},{4,12},{5,13},{6,14},{7,15},{8,16},{9,... | collective-permute-start | bytes 417800 | tf_op jit(solution)/shard_map/ppermute | solution.py:123
  8.9 1.6 %collective-permute-start.4 = (bf16[1,272,256]{2,1,0:T(8,128)(2,1)}, bf16[1,272,256]{2,1,0:T(8,128)(2,1)S(1)}, u32[]{:S(2)}, u32[]{:S(2)}) collective-permute-start(bf16[1,272,256]{2,1,0:T(8,128)(2,1)} %shard_map.77), channel_id=1, source_target_pairs={{0,25},{1,24},{2,27},{3,26},{4,15},{5,14},{6,13},{7,12},{8,17},{9,... | collective-permute-start | bytes 417800 | tf_op jit(solution)/shard_map/ppermute | solution.py:123
  10.5 1.1 %constant_dynamic-update-slice_fusion.7 = bf16[8,272,256]{2,1,0:T(8,128)(2,1)S(1)} fusion(bf16[1,272,256]{2,1,0:T(8,128)(2,1)} %shard_map.77), kind=kLoop, calls=%fused_computation.10 | loop fusion | bytes 278528
  11.6 0.0 collective-permute-done
  11.6 4.0 %collective-permute-start.5 = (bf16[1,272,256]{2,1,0:T(8,128)(2,1)}, bf16[1,272,256]{2,1,0:T(8,128)(2,1)S(1)}, u32[]{:S(2)}, u32[]{:S(2)}) collective-permute-start(bf16[1,272,256]{2,1,0:T(8,128)(2,1)} %shard_map.77), channel_id=1, source_target_pairs={{0,56},{1,57},{2,58},{3,59},{4,108},{5,109},{6,110},{7,111},{8,48}... | collective-permute-start | bytes 417800 | tf_op jit(solution)/shard_map/ppermute | solution.py:123
  15.6 0.0 collective-permute-done.1
  15.6 0.1 collective-permute-start.6
  15.7 0.0 collective-permute-done.2
  15.8 0.0 collective-permute-done.3
  15.8 0.5 collective-permute-done.4
  16.3 2.7 %collective-permute-done.5 = bf16[1,272,256]{2,1,0:T(8,128)(2,1)S(1)} collective-permute-done((bf16[1,272,256]{2,1,0:T(8,128)(2,1)}, bf16[1,272,256]{2,1,0:T(8,128)(2,1)S(1)}, u32[]{:S(2)}, u32[]{:S(2)}) %collective-permute-start.5) | collective-permute-done | bytes 139296 | tf_op jit(solution)/shard_map/ppermute | solution.py:123
  19.1 4.9 %collective-permute-done.6 = bf16[1,272,256]{2,1,0:T(8,128)(2,1)S(1)} collective-permute-done((bf16[1,272,256]{2,1,0:T(8,128)(2,1)}, bf16[1,272,256]{2,1,0:T(8,128)(2,1)S(1)}, u32[]{:S(2)}, u32[]{:S(2)}) %collective-permute-start.6) | collective-permute-done | bytes 139296 | tf_op jit(solution)/shard_map/ppermute | solution.py:123
  24.0 0.0 copy-start.1
  24.0 0.0 copy-start.2
  24.0 0.1 fusion
  24.1 0.1 collective-permute-start.7
  24.2 2.2 %collective-permute-start.8 = (bf16[8,96,256]{2,1,0:T(8,128)(2,1)S(1)}, bf16[8,96,256]{2,1,0:T(8,128)(2,1)S(1)}, u32[]{:S(2)}, u32[]{:S(2)}) collective-permute-start(bf16[8,96,256]{2,1,0:T(8,128)(2,1)S(1)} %get-tuple-element.32), channel_id=1, source_target_pairs={{0,96},{1,97},{2,98},{3,99},{4,36},{5,37},{6,38},{7,39},{8,104},{9... | collective-permute-start | bytes 1179656 | tf_op jit(solution)/shard_map/ppermute | solution.py:123
  26.4 2.7 %collective-permute-start.9 = (bf16[8,80,256]{2,1,0:T(8,128)(2,1)S(1)}, bf16[8,80,256]{2,1,0:T(8,128)(2,1)S(1)}, u32[]{:S(2)}, u32[]{:S(2)}) collective-permute-start(bf16[8,80,256]{2,1,0:T(8,128)(2,1)S(1)} %slice.11), channel_id=1, source_target_pairs={{0,3},{1,2},{2,1},{3,0},{4,5},{5,4},{6,7},{7,6},{8,11},{9,10},{10,... | collective-permute-start | bytes 983048 | tf_op jit(solution)/shard_map/ppermute | solution.py:123
  29.1 0.0 copy-done
  29.1 0.0 copy-done.1
  29.1 0.0 copy-done.2
  29.1 4.0 %shard_map.78 = (bf16[32,256,256]{2,1,0:T(8,128)(2,1)}, bf16[256,256]{1,0:T(8,128)(2,1)S(1)}, bf16[256,256]{1,0:T(8,128)(2,1)S(1)}) custom-call(bf16[3,3]{1,0:T(4,128)(2,1)S(1)} %copy-done.1, bf16[3,3]{1,0:T(4,128)(2,1)S(1)} %copy-done.2, bf16[32,256,256]{2,1,0:T(8,128)(2,1)S(1)} %copy-done), custom_call_target="tpu_custom_call" | custom-call | flops 16777216 | bytes 20971520 | tf_op jit(solution)/shard_map/pallas_call | solution.py:108
  33.1 1.6 %collective-permute-done.9 = bf16[8,80,256]{2,1,0:T(8,128)(2,1)S(1)} collective-permute-done((bf16[8,80,256]{2,1,0:T(8,128)(2,1)S(1)}, bf16[8,80,256]{2,1,0:T(8,128)(2,1)S(1)}, u32[]{:S(2)}, u32[]{:S(2)}) %collective-permute-start.9) | collective-permute-done | bytes 327712 | tf_op jit(solution)/shard_map/ppermute | solution.py:123
  34.8 0.0 collective-permute-done.7
  34.8 0.0 collective-permute-done.8
  34.8 0.0 collective-permute-start.13
  34.8 0.1 pad_maximum_fusion.2.refs_2_.refs_6_
  34.8 1.2 %collective-permute-start.12 = (bf16[16,80,256]{2,1,0:T(8,128)(2,1)S(1)}, bf16[16,80,256]{2,1,0:T(8,128)(2,1)S(1)}, u32[]{:S(2)}, u32[]{:S(2)}) collective-permute-start(bf16[16,80,256]{2,1,0:T(8,128)(2,1)S(1)} %pad_maximum_fusion.2.refs_2_.refs_6_), channel_id=1, source_target_pairs={{0,96},{1,97},{2,98},{3,99},{4,36},{5,37},{6,38},{7,39},{8,104},{9... | collective-permute-start | bytes 1966088 | tf_op jit(solution)/shard_map/ppermute | solution.py:123
  36.1 0.1 pad_maximum_fusion.1.refs_1_.refs_3_
  36.1 0.0 copy-start.5
  36.2 0.1 pad_maximum_fusion.refs_0_
  36.2 2.0 %collective-permute-start.11 = (bf16[16,96,256]{2,1,0:T(8,128)(2,1)S(1)}, bf16[16,96,256]{2,1,0:T(8,128)(2,1)S(1)}, u32[]{:S(2)}, u32[]{:S(2)}) collective-permute-start(bf16[16,96,256]{2,1,0:T(8,128)(2,1)S(1)} %pad_maximum_fusion.1.refs_1_.refs_3_), channel_id=1, source_target_pairs={{0,8},{1,9},{2,10},{3,11},{4,28},{5,29},{6,30},{7,31},{8,0},{9,1},... | collective-permute-start | bytes 2359304 | tf_op jit(solution)/shard_map/ppermute | solution.py:123
  38.2 2.5 %collective-permute-start.10 = (bf16[16,96,256]{2,1,0:T(8,128)(2,1)S(1)}, bf16[16,96,256]{2,1,0:T(8,128)(2,1)}, u32[]{:S(2)}, u32[]{:S(2)}) collective-permute-start(bf16[16,96,256]{2,1,0:T(8,128)(2,1)S(1)} %pad_maximum_fusion.refs_0_), channel_id=1, source_target_pairs={{0,3},{1,2},{2,1},{3,0},{4,5},{5,4},{6,7},{7,6},{8,11},{9,10},{10,... | collective-permute-start | bytes 2359304 | tf_op jit(solution)/shard_map/ppermute | solution.py:123
  40.8 0.7 collective-permute-start.16
  41.5 5.2 %collective-permute-done.12.refs_7_.refs_6_ = bf16[16,80,256]{2,1,0:T(8,128)(2,1)S(1)} collective-permute-done((bf16[16,80,256]{2,1,0:T(8,128)(2,1)S(1)}, bf16[16,80,256]{2,1,0:T(8,128)(2,1)S(1)}, u32[]{:S(2)}, u32[]{:S(2)}) %collective-permute-start.12) | collective-permute-done | bytes 655392 | tf_op jit(solution)/shard_map/ppermute | solution.py:123
  46.7 0.8 copy-done.3
  47.6 1.1 %collective-permute-start.14 = (bf16[16,96,256]{2,1,0:T(8,128)(2,1)S(1)}, bf16[16,96,256]{2,1,0:T(8,128)(2,1)}, u32[]{:S(2)}, u32[]{:S(2)}) collective-permute-start(bf16[16,96,256]{2,1,0:T(8,128)(2,1)S(1)} %pad_maximum_fusion.refs_0_), channel_id=1, source_target_pairs={{0,96},{1,97},{2,98},{3,99},{4,36},{5,37},{6,38},{7,39},{8,104},{9... | collective-permute-start | bytes 2359304 | tf_op jit(solution)/shard_map/ppermute | solution.py:123
  48.7 0.0 collective-permute-done.13.refs_4_
  48.7 1.9 %collective-permute-start.18 = (bf16[16,80,256]{2,1,0:T(8,128)(2,1)S(1)}, bf16[16,80,256]{2,1,0:T(8,128)(2,1)}, u32[]{:S(2)}, u32[]{:S(2)}) collective-permute-start(bf16[16,80,256]{2,1,0:T(8,128)(2,1)S(1)} %pad_maximum_fusion.2.refs_2_.refs_6_), channel_id=1, source_target_pairs={{0,8},{1,9},{2,10},{3,11},{4,28},{5,29},{6,30},{7,31},{8,0},{9,1},... | collective-permute-start | bytes 1966088 | tf_op jit(solution)/shard_map/ppermute | solution.py:123
  50.6 0.0 copy-done.5
  50.6 0.1 multiply_add_fusion
  50.7 0.1 reshape.62
  50.8 0.1 pad_add_fusion.place_ref
  50.9 7.0 %shard_map.79 = (f32[8,128]{1,0:T(8,128)S(1)}, bf16[64,256,256]{2,1,0:T(8,128)(2,1)S(1)}) custom-call(s32[66]{0:T(128)S(1)} %pad_add_fusion.place_ref, bf16[16,96,256]{2,1,0:T(8,128)(2,1)S(1)} %pad_maximum_fusion.refs_0_, bf16[16,96,256]{2,1,0:T(8,128)(2,1)S(1)} %pad_maximum_fusion.1.refs_1_.refs_3_, ...), custom_call_target="tpu_custom_call" | custom-call | flops 2415919104 | bytes 16777216 | tf_op jit(solution)/shard_map/pallas_call | solution.py:279
  57.9 0.0 collective-permute-done.11.refs_4_.refs_3_
  57.9 0.0 collective-permute-done.10.refs_1_.refs_0_
  58.0 2.2 %collective-permute-start.15 = (bf16[16,96,256]{2,1,0:T(8,128)(2,1)}, bf16[16,96,256]{2,1,0:T(8,128)(2,1)S(1)}, u32[]{:S(2)}, u32[]{:S(2)}) collective-permute-start(bf16[16,96,256]{2,1,0:T(8,128)(2,1)} %collective-permute-done.10.refs_1_.refs_0_), channel_id=1, source_target_pairs={{0,96},{1,97},{2,98},{3,99},{4,36},{5,37},{6,38},{7,39},{8,104},{9... | collective-permute-start | bytes 2359304 | tf_op jit(solution)/shard_map/ppermute | solution.py:123
  60.1 2.6 %collective-permute-start.17 = (bf16[16,96,256]{2,1,0:T(8,128)(2,1)S(1)}, bf16[16,96,256]{2,1,0:T(8,128)(2,1)S(1)}, u32[]{:S(2)}, u32[]{:S(2)}) collective-permute-start(bf16[16,96,256]{2,1,0:T(8,128)(2,1)S(1)} %collective-permute-done.11.refs_4_.refs_3_), channel_id=1, source_target_pairs={{0,3},{1,2},{2,1},{3,0},{4,5},{5,4},{6,7},{7,6},{8,11},{9,10},{10,... | collective-permute-start | bytes 2359304 | tf_op jit(solution)/shard_map/ppermute | solution.py:123
  62.7 0.0 collective-permute-done.18.refs_8_.refs_7_
  62.7 0.0 copy-done.4
  62.7 0.1 collective-permute-start.19
  62.8 0.0 collective-permute-done.16.refs_5_.refs_4_
  62.8 0.0 collective-permute-done.14.refs_2_.refs_1_
  62.8 10.8 %shard_map.80.refs_10_ = f32[24,128]{1,0:T(8,128)S(1)} custom-call(s32[66]{0:T(128)S(1)} %pad_add_fusion.place_ref, bf16[16,96,256]{2,1,0:T(8,128)(2,1)S(1)} %pad_maximum_fusion.refs_0_, bf16[16,96,256]{2,1,0:T(8,128)(2,1)} %collective-permute-done.10.refs_1_.refs_0_, bf16[16,96,256]{2,1,0:T(8,128)(2,1)} %collective-permute-done.14.refs_2_.refs_1_, ...), custom_call_target="tpu_custom_call" | custom-call | flops 7247757312 | bytes 16777216 | tf_op jit(solution)/shard_map/pallas_call | solution.py:279
  73.6 0.0 collective-permute-done.19.refs_8_
  73.6 0.0 collective-permute-done.15.refs_2_
  73.6 0.0 collective-permute-done.17.refs_5_
  73.6 12.0 %shard_map.81 = f32[64,128]{1,0:T(8,128)S(1)} custom-call(s32[66]{0:T(128)S(1)} %pad_add_fusion.place_ref, bf16[16,96,256]{2,1,0:T(8,128)(2,1)} %collective-permute-done.10.refs_1_.refs_0_, bf16[16,96,256]{2,1,0:T(8,128)(2,1)} %collective-permute-done.14.refs_2_.refs_1_, bf16[16,96,256]{2,1,0:T(8,128)(2,1)S(1)} %collective-permute-done.15.refs_2_, ...), custom_call_target="tpu_custom_call" | custom-call | flops 9663676416 | bytes 16777216 | tf_op jit(solution)/shard_map/pallas_call | solution.py:279
  85.6 15.7 %all_to_all.11 = f32[64,1,128]{2,1,0:T(1,128)} all-to-all(f32[64,1,128]{2,1,0:T(1,128)S(1)} %bitcast.6), channel_id=1, replica_groups=mesh['x'=4,'y'=4,'c'=2,'z'=4] {'x','y','z'}, dimensions={0} | all-to-all | bytes 65536 | tf_op jit(solution)/shard_map/all_to_all | solution.py:360
  101.3 1.5 %shard_map.82 = (f32[1,128]{1,0:T(1,128)}, f32[1,100]{1,0:T(1,128)}) custom-call(f32[64,128]{1,0:T(8,128)} %bitcast.7), custom_call_target="tpu_custom_call" | custom-call | tf_op jit(solution)/shard_map/pallas_call | solution.py:316
  (11 shorter events, 0.1 us)
Async XLA Ops:
  2.3 9.2 %collective-permute-start = (bf16[1,272,256]{2,1,0:T(8,128)(2,1)}, bf16[1,272,256]{2,1,0:T(8,128)(2,1)S(1)}, u32[]{:S(2)}, u32[]{:S(2)}) collective-permute-start(bf16[1,272,256]{2,1,0:T(8,128)(2,1)} %shard_map.77), channel_id=1, source_target_pairs={{0,1},{1,0},{2,3},{3,2},{4,7},{5,6},{6,5},{7,4},{8,9},{9,8},{10,11... | collective-permute-start | bytes 417800 | tf_op jit(solution)/shard_map/ppermute | solution.py:123
  4.3 11.3 %collective-permute-start.1 = (bf16[1,272,256]{2,1,0:T(8,128)(2,1)}, bf16[1,272,256]{2,1,0:T(8,128)(2,1)S(1)}, u32[]{:S(2)}, u32[]{:S(2)}) collective-permute-start(bf16[1,272,256]{2,1,0:T(8,128)(2,1)} %shard_map.77), channel_id=1, source_target_pairs={{0,32},{1,33},{2,34},{3,35},{4,100},{5,101},{6,102},{7,103},{8,40}... | collective-permute-start | bytes 417800 | tf_op jit(solution)/shard_map/ppermute | solution.py:123
  5.8 9.9 %collective-permute-start.2 = (bf16[1,272,256]{2,1,0:T(8,128)(2,1)}, bf16[1,272,256]{2,1,0:T(8,128)(2,1)S(1)}, u32[]{:S(2)}, u32[]{:S(2)}) collective-permute-start(bf16[1,272,256]{2,1,0:T(8,128)(2,1)} %shard_map.77), channel_id=1, source_target_pairs={{0,33},{1,32},{2,35},{3,34},{4,103},{5,102},{6,101},{7,100},{8,41}... | collective-permute-start | bytes 417800 | tf_op jit(solution)/shard_map/ppermute | solution.py:123
  5.8 9.9 %collective-permute-start.3 = (bf16[1,272,256]{2,1,0:T(8,128)(2,1)}, bf16[1,272,256]{2,1,0:T(8,128)(2,1)S(1)}, u32[]{:S(2)}, u32[]{:S(2)}) collective-permute-start(bf16[1,272,256]{2,1,0:T(8,128)(2,1)} %shard_map.77), channel_id=1, source_target_pairs={{0,24},{1,25},{2,26},{3,27},{4,12},{5,13},{6,14},{7,15},{8,16},{9,... | collective-permute-start | bytes 417800 | tf_op jit(solution)/shard_map/ppermute | solution.py:123
  8.9 7.4 %collective-permute-start.4 = (bf16[1,272,256]{2,1,0:T(8,128)(2,1)}, bf16[1,272,256]{2,1,0:T(8,128)(2,1)S(1)}, u32[]{:S(2)}, u32[]{:S(2)}) collective-permute-start(bf16[1,272,256]{2,1,0:T(8,128)(2,1)} %shard_map.77), channel_id=1, source_target_pairs={{0,25},{1,24},{2,27},{3,26},{4,15},{5,14},{6,13},{7,12},{8,17},{9,... | collective-permute-start | bytes 417800 | tf_op jit(solution)/shard_map/ppermute | solution.py:123
  10.5 18.6 %copy-start = (bf16[32,256,256]{2,1,0:T(8,128)(2,1)S(1)}, bf16[32,256,256]{2,1,0:T(8,128)(2,1)}, u32[]{:S(2)}) copy-start(bf16[32,256,256]{2,1,0:T(8,128)(2,1)} %maps_hbm) | copy-start | bytes 12582916
  11.6 7.5 %collective-permute-start.5 = (bf16[1,272,256]{2,1,0:T(8,128)(2,1)}, bf16[1,272,256]{2,1,0:T(8,128)(2,1)S(1)}, u32[]{:S(2)}, u32[]{:S(2)}) collective-permute-start(bf16[1,272,256]{2,1,0:T(8,128)(2,1)} %shard_map.77), channel_id=1, source_target_pairs={{0,56},{1,57},{2,58},{3,59},{4,108},{5,109},{6,110},{7,111},{8,48}... | collective-permute-start | bytes 417800 | tf_op jit(solution)/shard_map/ppermute | solution.py:123
  15.6 8.4 %collective-permute-start.6 = (bf16[1,272,256]{2,1,0:T(8,128)(2,1)}, bf16[1,272,256]{2,1,0:T(8,128)(2,1)S(1)}, u32[]{:S(2)}, u32[]{:S(2)}) collective-permute-start(bf16[1,272,256]{2,1,0:T(8,128)(2,1)} %shard_map.77), channel_id=1, source_target_pairs={{0,57},{1,56},{2,59},{3,58},{4,111},{5,110},{6,109},{7,108},{8,49}... | collective-permute-start | bytes 417800 | tf_op jit(solution)/shard_map/ppermute | solution.py:123
  24.0 5.1 %copy-start.1 = (bf16[3,3]{1,0:T(4,128)(2,1)S(1)}, bf16[3,3]{1,0:T(4,128)(2,1)}, u32[]{:S(2)}) copy-start(bf16[3,3]{1,0:T(4,128)(2,1)} %tap_q_ref.1) | copy-start | bytes 58
  24.0 5.0 %copy-start.2 = (bf16[3,3]{1,0:T(4,128)(2,1)S(1)}, bf16[3,3]{1,0:T(4,128)(2,1)}, u32[]{:S(2)}) copy-start(bf16[3,3]{1,0:T(4,128)(2,1)} %tap_d_ref.1) | copy-start | bytes 58
  24.1 10.7 %collective-permute-start.7 = (bf16[8,96,256]{2,1,0:T(8,128)(2,1)S(1)}, bf16[8,96,256]{2,1,0:T(8,128)(2,1)S(1)}, u32[]{:S(2)}, u32[]{:S(2)}) collective-permute-start(bf16[8,96,256]{2,1,0:T(8,128)(2,1)S(1)} %get-tuple-element.33), channel_id=1, source_target_pairs={{0,8},{1,9},{2,10},{3,11},{4,28},{5,29},{6,30},{7,31},{8,0},{9,1},... | collective-permute-start | bytes 1179656 | tf_op jit(solution)/shard_map/ppermute | solution.py:123
  24.2 10.6 %collective-permute-start.8 = (bf16[8,96,256]{2,1,0:T(8,128)(2,1)S(1)}, bf16[8,96,256]{2,1,0:T(8,128)(2,1)S(1)}, u32[]{:S(2)}, u32[]{:S(2)}) collective-permute-start(bf16[8,96,256]{2,1,0:T(8,128)(2,1)S(1)} %get-tuple-element.32), channel_id=1, source_target_pairs={{0,96},{1,97},{2,98},{3,99},{4,36},{5,37},{6,38},{7,39},{8,104},{9... | collective-permute-start | bytes 1179656 | tf_op jit(solution)/shard_map/ppermute | solution.py:123
  26.4 8.4 %collective-permute-start.9 = (bf16[8,80,256]{2,1,0:T(8,128)(2,1)S(1)}, bf16[8,80,256]{2,1,0:T(8,128)(2,1)S(1)}, u32[]{:S(2)}, u32[]{:S(2)}) collective-permute-start(bf16[8,80,256]{2,1,0:T(8,128)(2,1)S(1)} %slice.11), channel_id=1, source_target_pairs={{0,3},{1,2},{2,1},{3,0},{4,5},{5,4},{6,7},{7,6},{8,11},{9,10},{10,... | collective-permute-start | bytes 983048 | tf_op jit(solution)/shard_map/ppermute | solution.py:123
  34.8 13.9 %collective-permute-start.13 = (bf16[32,256,256]{2,1,0:T(8,128)(2,1)}, bf16[32,256,256]{2,1,0:T(8,128)(2,1)}, u32[]{:S(2)}, u32[]{:S(2)}) collective-permute-start(bf16[32,256,256]{2,1,0:T(8,128)(2,1)} %get-tuple-element.23.refs_3_), channel_id=1, source_target_pairs={{0,4},{4,0},{1,5},{5,1},{2,6},{6,2},{3,7},{7,3},{8,12},{12,8},{9,1... | collective-permute-start | bytes 12582920 | tf_op jit(solution)/shard_map/ppermute | solution.py:348
  34.8 11.9 %collective-permute-start.12 = (bf16[16,80,256]{2,1,0:T(8,128)(2,1)S(1)}, bf16[16,80,256]{2,1,0:T(8,128)(2,1)S(1)}, u32[]{:S(2)}, u32[]{:S(2)}) collective-permute-start(bf16[16,80,256]{2,1,0:T(8,128)(2,1)S(1)} %pad_maximum_fusion.2.refs_2_.refs_6_), channel_id=1, source_target_pairs={{0,96},{1,97},{2,98},{3,99},{4,36},{5,37},{6,38},{7,39},{8,104},{9... | collective-permute-start | bytes 1966088 | tf_op jit(solution)/shard_map/ppermute | solution.py:123
  36.1 14.5 %copy-start.5 = (s32[8]{0:T(128)S(1)}, s32[8]{0:T(128)}, u32[]{:S(2)}) copy-start(s32[8]{0:T(128)} %constant.41) | copy-start | bytes 100
  36.2 21.7 %collective-permute-start.11 = (bf16[16,96,256]{2,1,0:T(8,128)(2,1)S(1)}, bf16[16,96,256]{2,1,0:T(8,128)(2,1)S(1)}, u32[]{:S(2)}, u32[]{:S(2)}) collective-permute-start(bf16[16,96,256]{2,1,0:T(8,128)(2,1)S(1)} %pad_maximum_fusion.1.refs_1_.refs_3_), channel_id=1, source_target_pairs={{0,8},{1,9},{2,10},{3,11},{4,28},{5,29},{6,30},{7,31},{8,0},{9,1},... | collective-permute-start | bytes 2359304 | tf_op jit(solution)/shard_map/ppermute | solution.py:123
  38.2 19.7 %collective-permute-start.10 = (bf16[16,96,256]{2,1,0:T(8,128)(2,1)S(1)}, bf16[16,96,256]{2,1,0:T(8,128)(2,1)}, u32[]{:S(2)}, u32[]{:S(2)}) collective-permute-start(bf16[16,96,256]{2,1,0:T(8,128)(2,1)S(1)} %pad_maximum_fusion.refs_0_), channel_id=1, source_target_pairs={{0,3},{1,2},{2,1},{3,0},{4,5},{5,4},{6,7},{7,6},{8,11},{9,10},{10,... | collective-permute-start | bytes 2359304 | tf_op jit(solution)/shard_map/ppermute | solution.py:123
  40.8 22.0 %collective-permute-start.16 = (bf16[16,96,256]{2,1,0:T(8,128)(2,1)S(1)}, bf16[16,96,256]{2,1,0:T(8,128)(2,1)}, u32[]{:S(2)}, u32[]{:S(2)}) collective-permute-start(bf16[16,96,256]{2,1,0:T(8,128)(2,1)S(1)} %pad_maximum_fusion.1.refs_1_.refs_3_), channel_id=1, source_target_pairs={{0,3},{1,2},{2,1},{3,0},{4,5},{5,4},{6,7},{7,6},{8,11},{9,10},{10,... | collective-permute-start | bytes 2359304 | tf_op jit(solution)/shard_map/ppermute | solution.py:123
  46.7 0.8 copy-start.3
  47.6 15.2 %collective-permute-start.14 = (bf16[16,96,256]{2,1,0:T(8,128)(2,1)S(1)}, bf16[16,96,256]{2,1,0:T(8,128)(2,1)}, u32[]{:S(2)}, u32[]{:S(2)}) collective-permute-start(bf16[16,96,256]{2,1,0:T(8,128)(2,1)S(1)} %pad_maximum_fusion.refs_0_), channel_id=1, source_target_pairs={{0,96},{1,97},{2,98},{3,99},{4,36},{5,37},{6,38},{7,39},{8,104},{9... | collective-permute-start | bytes 2359304 | tf_op jit(solution)/shard_map/ppermute | solution.py:123
  48.7 14.0 %collective-permute-start.18 = (bf16[16,80,256]{2,1,0:T(8,128)(2,1)S(1)}, bf16[16,80,256]{2,1,0:T(8,128)(2,1)}, u32[]{:S(2)}, u32[]{:S(2)}) collective-permute-start(bf16[16,80,256]{2,1,0:T(8,128)(2,1)S(1)} %pad_maximum_fusion.2.refs_2_.refs_6_), channel_id=1, source_target_pairs={{0,8},{1,9},{2,10},{3,11},{4,28},{5,29},{6,30},{7,31},{8,0},{9,1},... | collective-permute-start | bytes 1966088 | tf_op jit(solution)/shard_map/ppermute | solution.py:123
  50.9 11.8 %copy-start.4 = (bf16[16,80,256]{2,1,0:T(8,128)(2,1)S(1)}, bf16[16,80,256]{2,1,0:T(8,128)(2,1)}, u32[]{:S(2)}) copy-start(bf16[16,80,256]{2,1,0:T(8,128)(2,1)} %copy-done.3) | copy-start | bytes 1966084
  58.0 15.6 %collective-permute-start.15 = (bf16[16,96,256]{2,1,0:T(8,128)(2,1)}, bf16[16,96,256]{2,1,0:T(8,128)(2,1)S(1)}, u32[]{:S(2)}, u32[]{:S(2)}) collective-permute-start(bf16[16,96,256]{2,1,0:T(8,128)(2,1)} %collective-permute-done.10.refs_1_.refs_0_), channel_id=1, source_target_pairs={{0,96},{1,97},{2,98},{3,99},{4,36},{5,37},{6,38},{7,39},{8,104},{9... | collective-permute-start | bytes 2359304 | tf_op jit(solution)/shard_map/ppermute | solution.py:123
  60.1 13.5 %collective-permute-start.17 = (bf16[16,96,256]{2,1,0:T(8,128)(2,1)S(1)}, bf16[16,96,256]{2,1,0:T(8,128)(2,1)S(1)}, u32[]{:S(2)}, u32[]{:S(2)}) collective-permute-start(bf16[16,96,256]{2,1,0:T(8,128)(2,1)S(1)} %collective-permute-done.11.refs_4_.refs_3_), channel_id=1, source_target_pairs={{0,3},{1,2},{2,1},{3,0},{4,5},{5,4},{6,7},{7,6},{8,11},{9,10},{10,... | collective-permute-start | bytes 2359304 | tf_op jit(solution)/shard_map/ppermute | solution.py:123
  62.7 10.9 %collective-permute-start.19 = (bf16[16,80,256]{2,1,0:T(8,128)(2,1)S(1)}, bf16[16,80,256]{2,1,0:T(8,128)(2,1)S(1)}, u32[]{:S(2)}, u32[]{:S(2)}) collective-permute-start(bf16[16,80,256]{2,1,0:T(8,128)(2,1)S(1)} %copy-done.4), channel_id=1, source_target_pairs={{0,8},{1,9},{2,10},{3,11},{4,28},{5,29},{6,30},{7,31},{8,0},{9,1},... | collective-permute-start | bytes 1966088 | tf_op jit(solution)/shard_map/ppermute | solution.py:123

commit v2 on v1

--- a/solution.py
+++ b/solution.py
@@ -14,7 +14,7 @@
 IMAGES = 32
 NODES = 64
 CUTS = (0, 80, 176, CELLS)
-LARGE = 16
+LARGE = 24
 SMALL = 8
 
 epsilon = 1e-06
@@ -214,7 +214,7 @@
             count = count + (image >= 0).astype(jnp.int32)
         return count
 
-    count = lax.fori_loop(0, held, fill, jnp.int32(0))
+    count = lax.fori_loop(0, held, fill, jnp.int32(0), unroll=8)
     for extra in range(LARGE):
         pair_s[count + extra] = spare * 64
     for copy in image_copies:

time: 104 us -> 103 us (level); the launches traced: 103 us -> 103 us
  Pallas kernels: 37 us -> 40.4 us
  blocking collectives: 15.7 us -> 14 us
    pallas_call x3, Pallas kernels: 29.7 us -> 33.2 us  [pair_scores(): pl.pallas_call(functools.partial(pair_kernel, wave, names), out_shape=out...]
    all_to_all x1, blocking collectives: 15.7 us -> 14 us  [body(): lax.all_to_all(scores, NODE, split_axis=0, concat_axis=0, tiled=True)]
  transfers between devices with their start and end apart: 20 -> 20, of which waited for: 5 -> 5; matrix products, arithmetic and copies ran while one was open for 2% -> 2% of each run, Pallas kernels for 21% -> 22%
where the time goes in v2:
time: 103 us
  Pallas kernels  40.4 us (39%)
  starting transfers between devices  30.6 us (30%)
  waiting for transfers between devices  15.1 us (15%)
  blocking collectives  14 us (14%)
  local copies, waits for them, and re-layouts  2.18 us (2%)
    pallas_call x3, Pallas kernels, pair_scores(): pl.pallas_call(functools.partial(pair_kernel, wave, names), out_shape=out...  33.2 us
    ppermute x19, starting transfers between devices, move(): return lax.ppermute(array, MAIN, PAIRS[step])  30.6 us
    ppermute x19, waiting for transfers between devices, move(): return lax.ppermute(array, MAIN, PAIRS[step])  15.1 us
    all_to_all x1, blocking collectives, body(): lax.all_to_all(scores, NODE, split_axis=0, concat_axis=0, tiled=True)  14 us
    pallas_call x1, Pallas kernels, prepare_images(): pl.pallas_call(images_kernel, in_specs=[vmem, vmem, pl.BlockSpec(memory_s...  4.04 us
  transfers between devices with their start and end apart: 20, of which 5 were waited for; matrix products, arithmetic and copies ran while one was open for 2% of the time, Pallas kernels for 22%

profile of v2, /device:TPU:0, one launch (start us, length us, event | category | flops | bytes accessed | tf_op | source)
XLA Modules:
  0.0 103.5 jit_solution(8663433324706141230)
XLA Ops:
  0.6 1.7 %shard_map.77 = bf16[1,272,256]{2,1,0:T(8,128)(2,1)} custom-call(bf16[1,256,256]{2,1,0:T(8,128)(2,1)} %query_ref.1, s32[1,128]{1,0:T(1,128)} %ids_ref.1), custom_call_target="tpu_custom_call" | custom-call | tf_op jit(solution)/shard_map/pallas_call | solution.py:71
  2.3 2.0 %collective-permute-start = (bf16[1,272,256]{2,1,0:T(8,128)(2,1)}, bf16[1,272,256]{2,1,0:T(8,128)(2,1)S(1)}, u32[]{:S(2)}, u32[]{:S(2)}) collective-permute-start(bf16[1,272,256]{2,1,0:T(8,128)(2,1)} %shard_map.77), channel_id=1, source_target_pairs={{0,1},{1,0},{2,3},{3,2},{4,7},{5,6},{6,5},{7,4},{8,9},{9,8},{10,11... | collective-permute-start | bytes 417800 | tf_op jit(solution)/shard_map/ppermute | solution.py:123
  4.3 1.5 %collective-permute-start.1 = (bf16[1,272,256]{2,1,0:T(8,128)(2,1)}, bf16[1,272,256]{2,1,0:T(8,128)(2,1)S(1)}, u32[]{:S(2)}, u32[]{:S(2)}) collective-permute-start(bf16[1,272,256]{2,1,0:T(8,128)(2,1)} %shard_map.77), channel_id=1, source_target_pairs={{0,32},{1,33},{2,34},{3,35},{4,100},{5,101},{6,102},{7,103},{8,40}... | collective-permute-start | bytes 417800 | tf_op jit(solution)/shard_map/ppermute | solution.py:123
  5.8 0.0 collective-permute-start.2
  5.8 3.1 %collective-permute-start.3 = (bf16[1,272,256]{2,1,0:T(8,128)(2,1)}, bf16[1,272,256]{2,1,0:T(8,128)(2,1)S(1)}, u32[]{:S(2)}, u32[]{:S(2)}) collective-permute-start(bf16[1,272,256]{2,1,0:T(8,128)(2,1)} %shard_map.77), channel_id=1, source_target_pairs={{0,24},{1,25},{2,26},{3,27},{4,12},{5,13},{6,14},{7,15},{8,16},{9,... | collective-permute-start | bytes 417800 | tf_op jit(solution)/shard_map/ppermute | solution.py:123
  8.9 1.6 %collective-permute-start.4 = (bf16[1,272,256]{2,1,0:T(8,128)(2,1)}, bf16[1,272,256]{2,1,0:T(8,128)(2,1)S(1)}, u32[]{:S(2)}, u32[]{:S(2)}) collective-permute-start(bf16[1,272,256]{2,1,0:T(8,128)(2,1)} %shard_map.77), channel_id=1, source_target_pairs={{0,25},{1,24},{2,27},{3,26},{4,15},{5,14},{6,13},{7,12},{8,17},{9,... | collective-permute-start | bytes 417800 | tf_op jit(solution)/shard_map/ppermute | solution.py:123
  10.5 1.1 %constant_dynamic-update-slice_fusion.7 = bf16[8,272,256]{2,1,0:T(8,128)(2,1)S(1)} fusion(bf16[1,272,256]{2,1,0:T(8,128)(2,1)} %shard_map.77), kind=kLoop, calls=%fused_computation.10 | loop fusion | bytes 278528
  11.6 0.0 collective-permute-done
  11.6 4.0 %collective-permute-start.5 = (bf16[1,272,256]{2,1,0:T(8,128)(2,1)}, bf16[1,272,256]{2,1,0:T(8,128)(2,1)S(1)}, u32[]{:S(2)}, u32[]{:S(2)}) collective-permute-start(bf16[1,272,256]{2,1,0:T(8,128)(2,1)} %shard_map.77), channel_id=1, source_target_pairs={{0,56},{1,57},{2,58},{3,59},{4,108},{5,109},{6,110},{7,111},{8,48}... | collective-permute-start | bytes 417800 | tf_op jit(solution)/shard_map/ppermute | solution.py:123
  15.6 0.0 collective-permute-done.1
  15.6 0.1 collective-permute-start.6
  15.7 0.0 collective-permute-done.2
  15.8 0.0 collective-permute-done.3
  15.8 0.5 collective-permute-done.4
  16.3 2.7 %collective-permute-done.5 = bf16[1,272,256]{2,1,0:T(8,128)(2,1)S(1)} collective-permute-done((bf16[1,272,256]{2,1,0:T(8,128)(2,1)}, bf16[1,272,256]{2,1,0:T(8,128)(2,1)S(1)}, u32[]{:S(2)}, u32[]{:S(2)}) %collective-permute-start.5) | collective-permute-done | bytes 139296 | tf_op jit(solution)/shard_map/ppermute | solution.py:123
  19.1 4.9 %collective-permute-done.6 = bf16[1,272,256]{2,1,0:T(8,128)(2,1)S(1)} collective-permute-done((bf16[1,272,256]{2,1,0:T(8,128)(2,1)}, bf16[1,272,256]{2,1,0:T(8,128)(2,1)S(1)}, u32[]{:S(2)}, u32[]{:S(2)}) %collective-permute-start.6) | collective-permute-done | bytes 139296 | tf_op jit(solution)/shard_map/ppermute | solution.py:123
  24.0 0.0 copy-start.1
  24.0 0.0 copy-start.2
  24.0 0.1 fusion
  24.1 0.1 collective-permute-start.7
  24.2 2.2 %collective-permute-start.8 = (bf16[8,96,256]{2,1,0:T(8,128)(2,1)S(1)}, bf16[8,96,256]{2,1,0:T(8,128)(2,1)S(1)}, u32[]{:S(2)}, u32[]{:S(2)}) collective-permute-start(bf16[8,96,256]{2,1,0:T(8,128)(2,1)S(1)} %get-tuple-element.32), channel_id=1, source_target_pairs={{0,96},{1,97},{2,98},{3,99},{4,36},{5,37},{6,38},{7,39},{8,104},{9... | collective-permute-start | bytes 1179656 | tf_op jit(solution)/shard_map/ppermute | solution.py:123
  26.4 2.7 %collective-permute-start.9 = (bf16[8,80,256]{2,1,0:T(8,128)(2,1)S(1)}, bf16[8,80,256]{2,1,0:T(8,128)(2,1)S(1)}, u32[]{:S(2)}, u32[]{:S(2)}) collective-permute-start(bf16[8,80,256]{2,1,0:T(8,128)(2,1)S(1)} %slice.11), channel_id=1, source_target_pairs={{0,3},{1,2},{2,1},{3,0},{4,5},{5,4},{6,7},{7,6},{8,11},{9,10},{10,... | collective-permute-start | bytes 983048 | tf_op jit(solution)/shard_map/ppermute | solution.py:123
  29.1 0.0 copy-done
  29.1 0.0 copy-done.1
  29.1 0.0 copy-done.2
  29.1 4.0 %shard_map.78 = (bf16[32,256,256]{2,1,0:T(8,128)(2,1)}, bf16[256,256]{1,0:T(8,128)(2,1)S(1)}, bf16[256,256]{1,0:T(8,128)(2,1)S(1)}) custom-call(bf16[3,3]{1,0:T(4,128)(2,1)S(1)} %copy-done.1, bf16[3,3]{1,0:T(4,128)(2,1)S(1)} %copy-done.2, bf16[32,256,256]{2,1,0:T(8,128)(2,1)S(1)} %copy-done), custom_call_target="tpu_custom_call" | custom-call | flops 16777216 | bytes 20971520 | tf_op jit(solution)/shard_map/pallas_call | solution.py:108
  33.1 1.6 %collective-permute-done.9 = bf16[8,80,256]{2,1,0:T(8,128)(2,1)S(1)} collective-permute-done((bf16[8,80,256]{2,1,0:T(8,128)(2,1)S(1)}, bf16[8,80,256]{2,1,0:T(8,128)(2,1)S(1)}, u32[]{:S(2)}, u32[]{:S(2)}) %collective-permute-start.9) | collective-permute-done | bytes 327712 | tf_op jit(solution)/shard_map/ppermute | solution.py:123
  34.8 0.0 collective-permute-done.7
  34.8 0.0 collective-permute-done.8
  34.8 0.0 collective-permute-start.13
  34.8 0.1 pad_maximum_fusion.2.refs_2_.refs_6_
  34.8 1.2 %collective-permute-start.12 = (bf16[16,80,256]{2,1,0:T(8,128)(2,1)S(1)}, bf16[16,80,256]{2,1,0:T(8,128)(2,1)S(1)}, u32[]{:S(2)}, u32[]{:S(2)}) collective-permute-start(bf16[16,80,256]{2,1,0:T(8,128)(2,1)S(1)} %pad_maximum_fusion.2.refs_2_.refs_6_), channel_id=1, source_target_pairs={{0,96},{1,97},{2,98},{3,99},{4,36},{5,37},{6,38},{7,39},{8,104},{9... | collective-permute-start | bytes 1966088 | tf_op jit(solution)/shard_map/ppermute | solution.py:123
  36.1 0.1 pad_maximum_fusion.1.refs_1_.refs_3_
  36.1 0.0 copy-start.5
  36.2 0.1 pad_maximum_fusion.refs_0_
  36.2 2.0 %collective-permute-start.11 = (bf16[16,96,256]{2,1,0:T(8,128)(2,1)S(1)}, bf16[16,96,256]{2,1,0:T(8,128)(2,1)S(1)}, u32[]{:S(2)}, u32[]{:S(2)}) collective-permute-start(bf16[16,96,256]{2,1,0:T(8,128)(2,1)S(1)} %pad_maximum_fusion.1.refs_1_.refs_3_), channel_id=1, source_target_pairs={{0,8},{1,9},{2,10},{3,11},{4,28},{5,29},{6,30},{7,31},{8,0},{9,1},... | collective-permute-start | bytes 2359304 | tf_op jit(solution)/shard_map/ppermute | solution.py:123
  38.2 2.5 %collective-permute-start.10 = (bf16[16,96,256]{2,1,0:T(8,128)(2,1)S(1)}, bf16[16,96,256]{2,1,0:T(8,128)(2,1)}, u32[]{:S(2)}, u32[]{:S(2)}) collective-permute-start(bf16[16,96,256]{2,1,0:T(8,128)(2,1)S(1)} %pad_maximum_fusion.refs_0_), channel_id=1, source_target_pairs={{0,3},{1,2},{2,1},{3,0},{4,5},{5,4},{6,7},{7,6},{8,11},{9,10},{10,... | collective-permute-start | bytes 2359304 | tf_op jit(solution)/shard_map/ppermute | solution.py:123
  40.8 0.7 collective-permute-start.16
  41.5 5.2 %collective-permute-done.12.refs_7_.refs_6_ = bf16[16,80,256]{2,1,0:T(8,128)(2,1)S(1)} collective-permute-done((bf16[16,80,256]{2,1,0:T(8,128)(2,1)S(1)}, bf16[16,80,256]{2,1,0:T(8,128)(2,1)S(1)}, u32[]{:S(2)}, u32[]{:S(2)}) %collective-permute-start.12) | collective-permute-done | bytes 655392 | tf_op jit(solution)/shard_map/ppermute | solution.py:123
  46.7 0.8 copy-done.3
  47.6 1.1 %collective-permute-start.14 = (bf16[16,96,256]{2,1,0:T(8,128)(2,1)S(1)}, bf16[16,96,256]{2,1,0:T(8,128)(2,1)}, u32[]{:S(2)}, u32[]{:S(2)}) collective-permute-start(bf16[16,96,256]{2,1,0:T(8,128)(2,1)S(1)} %pad_maximum_fusion.refs_0_), channel_id=1, source_target_pairs={{0,96},{1,97},{2,98},{3,99},{4,36},{5,37},{6,38},{7,39},{8,104},{9... | collective-permute-start | bytes 2359304 | tf_op jit(solution)/shard_map/ppermute | solution.py:123
  48.7 0.0 collective-permute-done.13.refs_4_
  48.7 1.9 %collective-permute-start.18 = (bf16[16,80,256]{2,1,0:T(8,128)(2,1)S(1)}, bf16[16,80,256]{2,1,0:T(8,128)(2,1)}, u32[]{:S(2)}, u32[]{:S(2)}) collective-permute-start(bf16[16,80,256]{2,1,0:T(8,128)(2,1)S(1)} %pad_maximum_fusion.2.refs_2_.refs_6_), channel_id=1, source_target_pairs={{0,8},{1,9},{2,10},{3,11},{4,28},{5,29},{6,30},{7,31},{8,0},{9,1},... | collective-permute-start | bytes 1966088 | tf_op jit(solution)/shard_map/ppermute | solution.py:123
  50.6 0.0 copy-done.5
  50.6 0.1 multiply_add_fusion
  50.7 0.1 reshape.62
  50.8 0.1 pad_add_fusion.place_ref
  50.9 7.9 %shard_map.79 = (f32[8,128]{1,0:T(8,128)S(1)}, bf16[64,256,256]{2,1,0:T(8,128)(2,1)S(1)}) custom-call(s32[66]{0:T(128)S(1)} %pad_add_fusion.place_ref, bf16[16,96,256]{2,1,0:T(8,128)(2,1)S(1)} %pad_maximum_fusion.refs_0_, bf16[16,96,256]{2,1,0:T(8,128)(2,1)S(1)} %pad_maximum_fusion.1.refs_1_.refs_3_, ...), custom_call_target="tpu_custom_call" | custom-call | flops 2415919104 | bytes 16777216 | tf_op jit(solution)/shard_map/pallas_call | solution.py:279
  58.8 0.0 collective-permute-done.11.refs_4_.refs_3_
  58.8 0.0 collective-permute-done.10.refs_1_.refs_0_
  58.8 1.2 %collective-permute-start.15 = (bf16[16,96,256]{2,1,0:T(8,128)(2,1)}, bf16[16,96,256]{2,1,0:T(8,128)(2,1)S(1)}, u32[]{:S(2)}, u32[]{:S(2)}) collective-permute-start(bf16[16,96,256]{2,1,0:T(8,128)(2,1)} %collective-permute-done.10.refs_1_.refs_0_), channel_id=1, source_target_pairs={{0,96},{1,97},{2,98},{3,99},{4,36},{5,37},{6,38},{7,39},{8,104},{9... | collective-permute-start | bytes 2359304 | tf_op jit(solution)/shard_map/ppermute | solution.py:123
  59.9 2.6 %collective-permute-start.17 = (bf16[16,96,256]{2,1,0:T(8,128)(2,1)S(1)}, bf16[16,96,256]{2,1,0:T(8,128)(2,1)S(1)}, u32[]{:S(2)}, u32[]{:S(2)}) collective-permute-start(bf16[16,96,256]{2,1,0:T(8,128)(2,1)S(1)} %collective-permute-done.11.refs_4_.refs_3_), channel_id=1, source_target_pairs={{0,3},{1,2},{2,1},{3,0},{4,5},{5,4},{6,7},{7,6},{8,11},{9,10},{10,... | collective-permute-start | bytes 2359304 | tf_op jit(solution)/shard_map/ppermute | solution.py:123
  62.5 0.0 collective-permute-done.18.refs_8_.refs_7_
  62.5 0.0 copy-done.4
  62.5 0.1 collective-permute-start.19
  62.6 0.0 collective-permute-done.16.refs_5_.refs_4_
  62.6 0.0 collective-permute-done.14.refs_2_.refs_1_
  62.6 11.2 %shard_map.80.refs_10_ = f32[24,128]{1,0:T(8,128)S(1)} custom-call(s32[66]{0:T(128)S(1)} %pad_add_fusion.place_ref, bf16[16,96,256]{2,1,0:T(8,128)(2,1)S(1)} %pad_maximum_fusion.refs_0_, bf16[16,96,256]{2,1,0:T(8,128)(2,1)} %collective-permute-done.10.refs_1_.refs_0_, bf16[16,96,256]{2,1,0:T(8,128)(2,1)} %collective-permute-done.14.refs_2_.refs_1_, ...), custom_call_target="tpu_custom_call" | custom-call | flops 7247757312 | bytes 16777216 | tf_op jit(solution)/shard_map/pallas_call | solution.py:279
  73.8 0.0 collective-permute-done.19.refs_8_
  73.8 0.0 collective-permute-done.15.refs_2_
  73.8 0.0 collective-permute-done.17.refs_5_
  73.8 14.2 %shard_map.81 = f32[64,128]{1,0:T(8,128)S(1)} custom-call(s32[66]{0:T(128)S(1)} %pad_add_fusion.place_ref, bf16[16,96,256]{2,1,0:T(8,128)(2,1)} %collective-permute-done.10.refs_1_.refs_0_, bf16[16,96,256]{2,1,0:T(8,128)(2,1)} %collective-permute-done.14.refs_2_.refs_1_, bf16[16,96,256]{2,1,0:T(8,128)(2,1)S(1)} %collective-permute-done.15.refs_2_, ...), custom_call_target="tpu_custom_call" | custom-call | flops 9663676416 | bytes 16777216 | tf_op jit(solution)/shard_map/pallas_call | solution.py:279
  88.0 14.0 %all_to_all.11 = f32[64,1,128]{2,1,0:T(1,128)} all-to-all(f32[64,1,128]{2,1,0:T(1,128)S(1)} %bitcast.6), channel_id=1, replica_groups=mesh['x'=4,'y'=4,'c'=2,'z'=4] {'x','y','z'}, dimensions={0} | all-to-all | bytes 65536 | tf_op jit(solution)/shard_map/all_to_all | solution.py:360
  102.0 1.5 %shard_map.82 = (f32[1,128]{1,0:T(1,128)}, f32[1,100]{1,0:T(1,128)}) custom-call(f32[64,128]{1,0:T(8,128)} %bitcast.7), custom_call_target="tpu_custom_call" | custom-call | tf_op jit(solution)/shard_map/pallas_call | solution.py:316
  (11 shorter events, 0.1 us)
Async XLA Ops:
  2.3 9.2 %collective-permute-start = (bf16[1,272,256]{2,1,0:T(8,128)(2,1)}, bf16[1,272,256]{2,1,0:T(8,128)(2,1)S(1)}, u32[]{:S(2)}, u32[]{:S(2)}) collective-permute-start(bf16[1,272,256]{2,1,0:T(8,128)(2,1)} %shard_map.77), channel_id=1, source_target_pairs={{0,1},{1,0},{2,3},{3,2},{4,7},{5,6},{6,5},{7,4},{8,9},{9,8},{10,11... | collective-permute-start | bytes 417800 | tf_op jit(solution)/shard_map/ppermute | solution.py:123
  4.3 11.3 %collective-permute-start.1 = (bf16[1,272,256]{2,1,0:T(8,128)(2,1)}, bf16[1,272,256]{2,1,0:T(8,128)(2,1)S(1)}, u32[]{:S(2)}, u32[]{:S(2)}) collective-permute-start(bf16[1,272,256]{2,1,0:T(8,128)(2,1)} %shard_map.77), channel_id=1, source_target_pairs={{0,32},{1,33},{2,34},{3,35},{4,100},{5,101},{6,102},{7,103},{8,40}... | collective-permute-start | bytes 417800 | tf_op jit(solution)/shard_map/ppermute | solution.py:123
  5.8 9.9 %collective-permute-start.2 = (bf16[1,272,256]{2,1,0:T(8,128)(2,1)}, bf16[1,272,256]{2,1,0:T(8,128)(2,1)S(1)}, u32[]{:S(2)}, u32[]{:S(2)}) collective-permute-start(bf16[1,272,256]{2,1,0:T(8,128)(2,1)} %shard_map.77), channel_id=1, source_target_pairs={{0,33},{1,32},{2,35},{3,34},{4,103},{5,102},{6,101},{7,100},{8,41}... | collective-permute-start | bytes 417800 | tf_op jit(solution)/shard_map/ppermute | solution.py:123
  5.8 9.9 %collective-permute-start.3 = (bf16[1,272,256]{2,1,0:T(8,128)(2,1)}, bf16[1,272,256]{2,1,0:T(8,128)(2,1)S(1)}, u32[]{:S(2)}, u32[]{:S(2)}) collective-permute-start(bf16[1,272,256]{2,1,0:T(8,128)(2,1)} %shard_map.77), channel_id=1, source_target_pairs={{0,24},{1,25},{2,26},{3,27},{4,12},{5,13},{6,14},{7,15},{8,16},{9,... | collective-permute-start | bytes 417800 | tf_op jit(solution)/shard_map/ppermute | solution.py:123
  8.9 7.4 %collective-permute-start.4 = (bf16[1,272,256]{2,1,0:T(8,128)(2,1)}, bf16[1,272,256]{2,1,0:T(8,128)(2,1)S(1)}, u32[]{:S(2)}, u32[]{:S(2)}) collective-permute-start(bf16[1,272,256]{2,1,0:T(8,128)(2,1)} %shard_map.77), channel_id=1, source_target_pairs={{0,25},{1,24},{2,27},{3,26},{4,15},{5,14},{6,13},{7,12},{8,17},{9,... | collective-permute-start | bytes 417800 | tf_op jit(solution)/shard_map/ppermute | solution.py:123
  10.5 18.6 %copy-start = (bf16[32,256,256]{2,1,0:T(8,128)(2,1)S(1)}, bf16[32,256,256]{2,1,0:T(8,128)(2,1)}, u32[]{:S(2)}) copy-start(bf16[32,256,256]{2,1,0:T(8,128)(2,1)} %maps_hbm) | copy-start | bytes 12582916
  11.6 7.5 %collective-permute-start.5 = (bf16[1,272,256]{2,1,0:T(8,128)(2,1)}, bf16[1,272,256]{2,1,0:T(8,128)(2,1)S(1)}, u32[]{:S(2)}, u32[]{:S(2)}) collective-permute-start(bf16[1,272,256]{2,1,0:T(8,128)(2,1)} %shard_map.77), channel_id=1, source_target_pairs={{0,56},{1,57},{2,58},{3,59},{4,108},{5,109},{6,110},{7,111},{8,48}... | collective-permute-start | bytes 417800 | tf_op jit(solution)/shard_map/ppermute | solution.py:123
  15.6 8.4 %collective-permute-start.6 = (bf16[1,272,256]{2,1,0:T(8,128)(2,1)}, bf16[1,272,256]{2,1,0:T(8,128)(2,1)S(1)}, u32[]{:S(2)}, u32[]{:S(2)}) collective-permute-start(bf16[1,272,256]{2,1,0:T(8,128)(2,1)} %shard_map.77), channel_id=1, source_target_pairs={{0,57},{1,56},{2,59},{3,58},{4,111},{5,110},{6,109},{7,108},{8,49}... | collective-permute-start | bytes 417800 | tf_op jit(solution)/shard_map/ppermute | solution.py:123
  24.0 5.1 %copy-start.1 = (bf16[3,3]{1,0:T(4,128)(2,1)S(1)}, bf16[3,3]{1,0:T(4,128)(2,1)}, u32[]{:S(2)}) copy-start(bf16[3,3]{1,0:T(4,128)(2,1)} %tap_q_ref.1) | copy-start | bytes 58
  24.0 5.0 %copy-start.2 = (bf16[3,3]{1,0:T(4,128)(2,1)S(1)}, bf16[3,3]{1,0:T(4,128)(2,1)}, u32[]{:S(2)}) copy-start(bf16[3,3]{1,0:T(4,128)(2,1)} %tap_d_ref.1) | copy-start | bytes 58
  24.1 10.7 %collective-permute-start.7 = (bf16[8,96,256]{2,1,0:T(8,128)(2,1)S(1)}, bf16[8,96,256]{2,1,0:T(8,128)(2,1)S(1)}, u32[]{:S(2)}, u32[]{:S(2)}) collective-permute-start(bf16[8,96,256]{2,1,0:T(8,128)(2,1)S(1)} %get-tuple-element.33), channel_id=1, source_target_pairs={{0,8},{1,9},{2,10},{3,11},{4,28},{5,29},{6,30},{7,31},{8,0},{9,1},... | collective-permute-start | bytes 1179656 | tf_op jit(solution)/shard_map/ppermute | solution.py:123
  24.2 10.6 %collective-permute-start.8 = (bf16[8,96,256]{2,1,0:T(8,128)(2,1)S(1)}, bf16[8,96,256]{2,1,0:T(8,128)(2,1)S(1)}, u32[]{:S(2)}, u32[]{:S(2)}) collective-permute-start(bf16[8,96,256]{2,1,0:T(8,128)(2,1)S(1)} %get-tuple-element.32), channel_id=1, source_target_pairs={{0,96},{1,97},{2,98},{3,99},{4,36},{5,37},{6,38},{7,39},{8,104},{9... | collective-permute-start | bytes 1179656 | tf_op jit(solution)/shard_map/ppermute | solution.py:123
  26.4 8.4 %collective-permute-start.9 = (bf16[8,80,256]{2,1,0:T(8,128)(2,1)S(1)}, bf16[8,80,256]{2,1,0:T(8,128)(2,1)S(1)}, u32[]{:S(2)}, u32[]{:S(2)}) collective-permute-start(bf16[8,80,256]{2,1,0:T(8,128)(2,1)S(1)} %slice.11), channel_id=1, source_target_pairs={{0,3},{1,2},{2,1},{3,0},{4,5},{5,4},{6,7},{7,6},{8,11},{9,10},{10,... | collective-permute-start | bytes 983048 | tf_op jit(solution)/shard_map/ppermute | solution.py:123
  34.8 13.9 %collective-permute-start.13 = (bf16[32,256,256]{2,1,0:T(8,128)(2,1)}, bf16[32,256,256]{2,1,0:T(8,128)(2,1)}, u32[]{:S(2)}, u32[]{:S(2)}) collective-permute-start(bf16[32,256,256]{2,1,0:T(8,128)(2,1)} %get-tuple-element.23.refs_3_), channel_id=1, source_target_pairs={{0,4},{4,0},{1,5},{5,1},{2,6},{6,2},{3,7},{7,3},{8,12},{12,8},{9,1... | collective-permute-start | bytes 12582920 | tf_op jit(solution)/shard_map/ppermute | solution.py:348
  34.8 11.9 %collective-permute-start.12 = (bf16[16,80,256]{2,1,0:T(8,128)(2,1)S(1)}, bf16[16,80,256]{2,1,0:T(8,128)(2,1)S(1)}, u32[]{:S(2)}, u32[]{:S(2)}) collective-permute-start(bf16[16,80,256]{2,1,0:T(8,128)(2,1)S(1)} %pad_maximum_fusion.2.refs_2_.refs_6_), channel_id=1, source_target_pairs={{0,96},{1,97},{2,98},{3,99},{4,36},{5,37},{6,38},{7,39},{8,104},{9... | collective-permute-start | bytes 1966088 | tf_op jit(solution)/shard_map/ppermute | solution.py:123
  36.1 14.5 %copy-start.5 = (s32[8]{0:T(128)S(1)}, s32[8]{0:T(128)}, u32[]{:S(2)}) copy-start(s32[8]{0:T(128)} %constant.41) | copy-start | bytes 100
  36.2 22.5 %collective-permute-start.11 = (bf16[16,96,256]{2,1,0:T(8,128)(2,1)S(1)}, bf16[16,96,256]{2,1,0:T(8,128)(2,1)S(1)}, u32[]{:S(2)}, u32[]{:S(2)}) collective-permute-start(bf16[16,96,256]{2,1,0:T(8,128)(2,1)S(1)} %pad_maximum_fusion.1.refs_1_.refs_3_), channel_id=1, source_target_pairs={{0,8},{1,9},{2,10},{3,11},{4,28},{5,29},{6,30},{7,31},{8,0},{9,1},... | collective-permute-start | bytes 2359304 | tf_op jit(solution)/shard_map/ppermute | solution.py:123
  38.2 20.5 %collective-permute-start.10 = (bf16[16,96,256]{2,1,0:T(8,128)(2,1)S(1)}, bf16[16,96,256]{2,1,0:T(8,128)(2,1)}, u32[]{:S(2)}, u32[]{:S(2)}) collective-permute-start(bf16[16,96,256]{2,1,0:T(8,128)(2,1)S(1)} %pad_maximum_fusion.refs_0_), channel_id=1, source_target_pairs={{0,3},{1,2},{2,1},{3,0},{4,5},{5,4},{6,7},{7,6},{8,11},{9,10},{10,... | collective-permute-start | bytes 2359304 | tf_op jit(solution)/shard_map/ppermute | solution.py:123
  40.8 21.9 %collective-permute-start.16 = (bf16[16,96,256]{2,1,0:T(8,128)(2,1)S(1)}, bf16[16,96,256]{2,1,0:T(8,128)(2,1)}, u32[]{:S(2)}, u32[]{:S(2)}) collective-permute-start(bf16[16,96,256]{2,1,0:T(8,128)(2,1)S(1)} %pad_maximum_fusion.1.refs_1_.refs_3_), channel_id=1, source_target_pairs={{0,3},{1,2},{2,1},{3,0},{4,5},{5,4},{6,7},{7,6},{8,11},{9,10},{10,... | collective-permute-start | bytes 2359304 | tf_op jit(solution)/shard_map/ppermute | solution.py:123
  46.7 0.8 copy-start.3
  47.6 15.1 %collective-permute-start.14 = (bf16[16,96,256]{2,1,0:T(8,128)(2,1)S(1)}, bf16[16,96,256]{2,1,0:T(8,128)(2,1)}, u32[]{:S(2)}, u32[]{:S(2)}) collective-permute-start(bf16[16,96,256]{2,1,0:T(8,128)(2,1)S(1)} %pad_maximum_fusion.refs_0_), channel_id=1, source_target_pairs={{0,96},{1,97},{2,98},{3,99},{4,36},{5,37},{6,38},{7,39},{8,104},{9... | collective-permute-start | bytes 2359304 | tf_op jit(solution)/shard_map/ppermute | solution.py:123
  48.7 13.8 %collective-permute-start.18 = (bf16[16,80,256]{2,1,0:T(8,128)(2,1)S(1)}, bf16[16,80,256]{2,1,0:T(8,128)(2,1)}, u32[]{:S(2)}, u32[]{:S(2)}) collective-permute-start(bf16[16,80,256]{2,1,0:T(8,128)(2,1)S(1)} %pad_maximum_fusion.2.refs_2_.refs_6_), channel_id=1, source_target_pairs={{0,8},{1,9},{2,10},{3,11},{4,28},{5,29},{6,30},{7,31},{8,0},{9,1},... | collective-permute-start | bytes 1966088 | tf_op jit(solution)/shard_map/ppermute | solution.py:123
  50.9 11.6 %copy-start.4 = (bf16[16,80,256]{2,1,0:T(8,128)(2,1)S(1)}, bf16[16,80,256]{2,1,0:T(8,128)(2,1)}, u32[]{:S(2)}) copy-start(bf16[16,80,256]{2,1,0:T(8,128)(2,1)} %copy-done.3) | copy-start | bytes 1966084
  58.8 15.0 %collective-permute-start.15 = (bf16[16,96,256]{2,1,0:T(8,128)(2,1)}, bf16[16,96,256]{2,1,0:T(8,128)(2,1)S(1)}, u32[]{:S(2)}, u32[]{:S(2)}) collective-permute-start(bf16[16,96,256]{2,1,0:T(8,128)(2,1)} %collective-permute-done.10.refs_1_.refs_0_), channel_id=1, source_target_pairs={{0,96},{1,97},{2,98},{3,99},{4,36},{5,37},{6,38},{7,39},{8,104},{9... | collective-permute-start | bytes 2359304 | tf_op jit(solution)/shard_map/ppermute | solution.py:123
  59.9 13.9 %collective-permute-start.17 = (bf16[16,96,256]{2,1,0:T(8,128)(2,1)S(1)}, bf16[16,96,256]{2,1,0:T(8,128)(2,1)S(1)}, u32[]{:S(2)}, u32[]{:S(2)}) collective-permute-start(bf16[16,96,256]{2,1,0:T(8,128)(2,1)S(1)} %collective-permute-done.11.refs_4_.refs_3_), channel_id=1, source_target_pairs={{0,3},{1,2},{2,1},{3,0},{4,5},{5,4},{6,7},{7,6},{8,11},{9,10},{10,... | collective-permute-start | bytes 2359304 | tf_op jit(solution)/shard_map/ppermute | solution.py:123
  62.5 11.3 %collective-permute-start.19 = (bf16[16,80,256]{2,1,0:T(8,128)(2,1)S(1)}, bf16[16,80,256]{2,1,0:T(8,128)(2,1)S(1)}, u32[]{:S(2)}, u32[]{:S(2)}) collective-permute-start(bf16[16,80,256]{2,1,0:T(8,128)(2,1)S(1)} %copy-done.4), channel_id=1, source_target_pairs={{0,8},{1,9},{2,10},{3,11},{4,28},{5,29},{6,30},{7,31},{8,0},{9,1},... | collective-permute-start | bytes 1966088 | tf_op jit(solution)/shard_map/ppermute | solution.py:123

commit v3 on v2

--- a/solution.py
+++ b/solution.py
@@ -133,8 +133,9 @@
         first = CUTS[piece] + (16 if piece else 0)
         pieces.append(held[:, first : CUTS[piece + 1] + 16])
     came = [move(p, o[0]) for p, o in zip(pieces, orders())]
-    *came, own = lax.optimization_barrier((*came, own))
-    return [jnp.concatenate(pair, axis=0) for pair in zip(pieces, came)], own
+    pieces = [jnp.concatenate(pair, axis=0) for pair in zip(pieces, came)]
+    pieces[0], own = lax.optimization_barrier((pieces[0], own))
+    return pieces, own
 
 
 def sources(combo):

time: 103 us -> 118 us (1.15); the launches traced: 103 us -> 116 us
  waiting for transfers between devices: 15.1 us -> 33.2 us
  Pallas kernels: 40.4 us -> 35 us
  starting transfers between devices: 30.6 us -> 28.5 us
  local copies, waits for them, and re-layouts: 2.18 us -> 4.25 us
    ppermute x19, waiting for transfers between devices: 15.1 us -> 33.2 us  [move(): return lax.ppermute(array, MAIN, PAIRS[step])]
    pallas_call x3, Pallas kernels: 33.2 us -> 27.8 us  [pair_scores(): pl.pallas_call(functools.partial(pair_kernel, wave, names), out_shape=out...]
    ppermute x19, starting transfers between devices: 30.6 us -> 26.6 us  [move(): return lax.ppermute(array, MAIN, PAIRS[step])]
    unnamed x19, local copies, waits for them, and re-layouts: 2 us -> 4.06 us
    ppermute x1, starting transfers between devices: 0.01 us -> 1.84 us  [body(): other = lax.ppermute(own, 'c', [(0, 1), (1, 0)])]
  transfers between devices with their start and end apart: 20 -> 20, of which waited for: 5 -> 8; matrix products, arithmetic and copies ran while one was open for 2% -> 1% of each run, Pallas kernels for 22% -> 17%
where the time goes in v3:
time: 118 us; the launch traced here: 116 us
  Pallas kernels  35 us (30%)
  waiting for transfers between devices  33.2 us (28%)
  starting transfers between devices  28.5 us (24%)
  blocking collectives  14.3 us (12%)
  local copies, waits for them, and re-layouts  4.25 us (4%)
    ppermute x19, waiting for transfers between devices, move(): return lax.ppermute(array, MAIN, PAIRS[step])  33.2 us
    pallas_call x3, Pallas kernels, pair_scores(): pl.pallas_call(functools.partial(pair_kernel, wave, names), out_shape=out...  27.8 us
    ppermute x19, starting transfers between devices, move(): return lax.ppermute(array, MAIN, PAIRS[step])  26.6 us
    all_to_all x1, blocking collectives, body(): lax.all_to_all(scores, NODE, split_axis=0, concat_axis=0, tiled=True)  14.3 us
    unnamed x19, local copies, waits for them, and re-layouts  4.06 us
    pallas_call x1, Pallas kernels, prepare_images(): pl.pallas_call(images_kernel, in_specs=[vmem, vmem, pl.BlockSpec(memory_s...  4.04 us
  transfers between devices with their start and end apart: 20, of which 8 were waited for; matrix products, arithmetic and copies ran while one was open for 1% of the time, Pallas kernels for 17%

profile of v3, /device:TPU:0, one launch (start us, length us, event | category | flops | bytes accessed | tf_op | source)
XLA Modules:
  0.0 116.4 jit_solution(9535242002024049210)
XLA Ops:
  0.6 1.7 %shard_map.77 = bf16[1,272,256]{2,1,0:T(8,128)(2,1)} custom-call(bf16[1,256,256]{2,1,0:T(8,128)(2,1)} %query_ref.1, s32[1,128]{1,0:T(1,128)} %ids_ref.1), custom_call_target="tpu_custom_call" | custom-call | tf_op jit(solution)/shard_map/pallas_call | solution.py:71
  2.3 2.0 %collective-permute-start = (bf16[1,272,256]{2,1,0:T(8,128)(2,1)}, bf16[1,272,256]{2,1,0:T(8,128)(2,1)S(1)}, u32[]{:S(2)}, u32[]{:S(2)}) collective-permute-start(bf16[1,272,256]{2,1,0:T(8,128)(2,1)} %shard_map.77), channel_id=1, source_target_pairs={{0,1},{1,0},{2,3},{3,2},{4,7},{5,6},{6,5},{7,4},{8,9},{9,8},{10,11... | collective-permute-start | bytes 417800 | tf_op jit(solution)/shard_map/ppermute | solution.py:123
  4.3 1.5 %collective-permute-start.1 = (bf16[1,272,256]{2,1,0:T(8,128)(2,1)}, bf16[1,272,256]{2,1,0:T(8,128)(2,1)S(1)}, u32[]{:S(2)}, u32[]{:S(2)}) collective-permute-start(bf16[1,272,256]{2,1,0:T(8,128)(2,1)} %shard_map.77), channel_id=1, source_target_pairs={{0,32},{1,33},{2,34},{3,35},{4,100},{5,101},{6,102},{7,103},{8,40}... | collective-permute-start | bytes 417800 | tf_op jit(solution)/shard_map/ppermute | solution.py:123
  5.8 0.0 collective-permute-start.2
  5.8 3.1 %collective-permute-start.3 = (bf16[1,272,256]{2,1,0:T(8,128)(2,1)}, bf16[1,272,256]{2,1,0:T(8,128)(2,1)S(1)}, u32[]{:S(2)}, u32[]{:S(2)}) collective-permute-start(bf16[1,272,256]{2,1,0:T(8,128)(2,1)} %shard_map.77), channel_id=1, source_target_pairs={{0,24},{1,25},{2,26},{3,27},{4,12},{5,13},{6,14},{7,15},{8,16},{9,... | collective-permute-start | bytes 417800 | tf_op jit(solution)/shard_map/ppermute | solution.py:123
  8.9 1.6 %collective-permute-start.4 = (bf16[1,272,256]{2,1,0:T(8,128)(2,1)}, bf16[1,272,256]{2,1,0:T(8,128)(2,1)S(1)}, u32[]{:S(2)}, u32[]{:S(2)}) collective-permute-start(bf16[1,272,256]{2,1,0:T(8,128)(2,1)} %shard_map.77), channel_id=1, source_target_pairs={{0,25},{1,24},{2,27},{3,26},{4,15},{5,14},{6,13},{7,12},{8,17},{9,... | collective-permute-start | bytes 417800 | tf_op jit(solution)/shard_map/ppermute | solution.py:123
  10.5 0.9 constant_dynamic-update-slice_fusion.7
  11.5 0.0 collective-permute-done
  11.5 4.0 %collective-permute-start.5 = (bf16[1,272,256]{2,1,0:T(8,128)(2,1)}, bf16[1,272,256]{2,1,0:T(8,128)(2,1)S(1)}, u32[]{:S(2)}, u32[]{:S(2)}) collective-permute-start(bf16[1,272,256]{2,1,0:T(8,128)(2,1)} %shard_map.77), channel_id=1, source_target_pairs={{0,56},{1,57},{2,58},{3,59},{4,108},{5,109},{6,110},{7,111},{8,48}... | collective-permute-start | bytes 417800 | tf_op jit(solution)/shard_map/ppermute | solution.py:123
  15.5 0.0 collective-permute-done.1
  15.5 0.1 collective-permute-start.6
  15.6 0.0 collective-permute-done.2
  15.7 0.0 collective-permute-done.3
  15.7 0.6 collective-permute-done.4
  16.3 0.0 copy-start.1
  16.3 0.0 copy-start.2
  16.3 2.6 %collective-permute-done.5 = bf16[1,272,256]{2,1,0:T(8,128)(2,1)S(1)} collective-permute-done((bf16[1,272,256]{2,1,0:T(8,128)(2,1)}, bf16[1,272,256]{2,1,0:T(8,128)(2,1)S(1)}, u32[]{:S(2)}, u32[]{:S(2)}) %collective-permute-start.5) | collective-permute-done | bytes 139296 | tf_op jit(solution)/shard_map/ppermute | solution.py:123
  18.9 4.9 %collective-permute-done.6 = bf16[1,272,256]{2,1,0:T(8,128)(2,1)S(1)} collective-permute-done((bf16[1,272,256]{2,1,0:T(8,128)(2,1)}, bf16[1,272,256]{2,1,0:T(8,128)(2,1)S(1)}, u32[]{:S(2)}, u32[]{:S(2)}) %collective-permute-start.6) | collective-permute-done | bytes 139296 | tf_op jit(solution)/shard_map/ppermute | solution.py:123
  23.9 0.1 fusion
  24.0 0.1 collective-permute-start.7
  24.1 0.0 copy-done.1
  24.1 0.0 copy-done.2
  24.1 0.0 copy-start
  24.1 2.2 %copy-done = bf16[32,256,256]{2,1,0:T(8,128)(2,1)S(1)} copy-done((bf16[32,256,256]{2,1,0:T(8,128)(2,1)S(1)}, bf16[32,256,256]{2,1,0:T(8,128)(2,1)}, u32[]{:S(2)}) %copy-start) | copy-done | bytes 4194328
  26.3 4.0 %shard_map.78 = (bf16[32,256,256]{2,1,0:T(8,128)(2,1)}, bf16[256,256]{1,0:T(8,128)(2,1)S(1)}, bf16[256,256]{1,0:T(8,128)(2,1)S(1)}) custom-call(bf16[3,3]{1,0:T(4,128)(2,1)S(1)} %copy-done.1, bf16[3,3]{1,0:T(4,128)(2,1)S(1)} %copy-done.2, bf16[32,256,256]{2,1,0:T(8,128)(2,1)S(1)} %copy-done), custom_call_target="tpu_custom_call" | custom-call | flops 16777216 | bytes 20971520 | tf_op jit(solution)/shard_map/pallas_call | solution.py:108
  30.3 1.5 %collective-permute-done.7 = bf16[8,96,256]{2,1,0:T(8,128)(2,1)S(1)} collective-permute-done((bf16[8,96,256]{2,1,0:T(8,128)(2,1)S(1)}, bf16[8,96,256]{2,1,0:T(8,128)(2,1)S(1)}, u32[]{:S(2)}, u32[]{:S(2)}) %collective-permute-start.7) | collective-permute-done | bytes 393248 | tf_op jit(solution)/shard_map/ppermute | solution.py:123
  31.8 0.1 pad_maximum_fusion.refs_0_
  31.9 1.8 %collective-permute-start.13 = (bf16[32,256,256]{2,1,0:T(8,128)(2,1)}, bf16[32,256,256]{2,1,0:T(8,128)(2,1)}, u32[]{:S(2)}, u32[]{:S(2)}) collective-permute-start(bf16[32,256,256]{2,1,0:T(8,128)(2,1)} %get-tuple-element.19.refs_3_), channel_id=1, source_target_pairs={{0,4},{4,0},{1,5},{5,1},{2,6},{6,2},{3,7},{7,3},{8,12},{12,8},{9,1... | collective-permute-start | bytes 12582920 | tf_op jit(solution)/shard_map/ppermute | solution.py:349
  33.8 0.9 collective-permute-start.11
  34.6 7.5 %collective-permute-done.11 = bf16[8,80,256]{2,1,0:T(8,128)(2,1)S(1)} collective-permute-done((bf16[8,80,256]{2,1,0:T(8,128)(2,1)S(1)}, bf16[8,80,256]{2,1,0:T(8,128)(2,1)S(1)}, u32[]{:S(2)}, u32[]{:S(2)}) %collective-permute-start.11) | collective-permute-done | bytes 327712 | tf_op jit(solution)/shard_map/ppermute | solution.py:123
  42.1 0.1 pad_maximum_fusion.2.refs_2_.refs_6_
  42.2 0.0 copy-start.5
  42.2 0.6 collective-permute-start.12
  42.8 2.8 %collective-permute-start.9 = (bf16[8,96,256]{2,1,0:T(8,128)(2,1)S(1)}, bf16[8,96,256]{2,1,0:T(8,128)(2,1)S(1)}, u32[]{:S(2)}, u32[]{:S(2)}) collective-permute-start(bf16[8,96,256]{2,1,0:T(8,128)(2,1)S(1)} %get-tuple-element.28), channel_id=1, source_target_pairs={{0,96},{1,97},{2,98},{3,99},{4,36},{5,37},{6,38},{7,39},{8,104},{9... | collective-permute-start | bytes 1179656 | tf_op jit(solution)/shard_map/ppermute | solution.py:123
  45.5 0.8 collective-permute-start.8
  46.3 12.0 %collective-permute-done.9 = bf16[8,96,256]{2,1,0:T(8,128)(2,1)S(1)} collective-permute-done((bf16[8,96,256]{2,1,0:T(8,128)(2,1)S(1)}, bf16[8,96,256]{2,1,0:T(8,128)(2,1)S(1)}, u32[]{:S(2)}, u32[]{:S(2)}) %collective-permute-start.9) | collective-permute-done | bytes 393248 | tf_op jit(solution)/shard_map/ppermute | solution.py:123
  58.3 0.1 pad_maximum_fusion.1.refs_1_.refs_3_
  58.4 0.8 collective-permute-start.10
  59.1 0.5 collective-permute-start.14
  59.6 0.0 collective-permute-done.12.refs_7_.refs_6_
  59.6 0.8 copy-done.3
  60.4 2.3 %collective-permute-start.16 = (bf16[16,96,256]{2,1,0:T(8,128)(2,1)S(1)}, bf16[16,96,256]{2,1,0:T(8,128)(2,1)}, u32[]{:S(2)}, u32[]{:S(2)}) collective-permute-start(bf16[16,96,256]{2,1,0:T(8,128)(2,1)S(1)} %pad_maximum_fusion.1.refs_1_.refs_3_), channel_id=1, source_target_pairs={{0,3},{1,2},{2,1},{3,0},{4,5},{5,4},{6,7},{7,6},{8,11},{9,10},{10,... | collective-permute-start | bytes 2359304 | tf_op jit(solution)/shard_map/ppermute | solution.py:123
  62.7 0.0 collective-permute-done.13.refs_4_
  62.7 1.5 %collective-permute-start.18 = (bf16[16,80,256]{2,1,0:T(8,128)(2,1)S(1)}, bf16[16,80,256]{2,1,0:T(8,128)(2,1)}, u32[]{:S(2)}, u32[]{:S(2)}) collective-permute-start(bf16[16,80,256]{2,1,0:T(8,128)(2,1)S(1)} %pad_maximum_fusion.2.refs_2_.refs_6_), channel_id=1, source_target_pairs={{0,8},{1,9},{2,10},{3,11},{4,28},{5,29},{6,30},{7,31},{8,0},{9,1},... | collective-permute-start | bytes 1966088 | tf_op jit(solution)/shard_map/ppermute | solution.py:123
  64.3 0.0 copy-done.5
  64.3 0.1 multiply_add_fusion
  64.3 0.1 reshape.62
  64.4 0.1 pad_add_fusion.place_ref
  64.5 6.8 %shard_map.79 = (f32[8,128]{1,0:T(8,128)S(1)}, bf16[64,256,256]{2,1,0:T(8,128)(2,1)S(1)}) custom-call(s32[66]{0:T(128)S(1)} %pad_add_fusion.place_ref, bf16[16,96,256]{2,1,0:T(8,128)(2,1)S(1)} %pad_maximum_fusion.refs_0_, bf16[16,96,256]{2,1,0:T(8,128)(2,1)S(1)} %pad_maximum_fusion.1.refs_1_.refs_3_, ...), custom_call_target="tpu_custom_call" | custom-call | flops 2415919104 | bytes 16777216 | tf_op jit(solution)/shard_map/pallas_call | solution.py:280
  71.4 0.0 collective-permute-done.8.refs_1_.refs_0_
  71.4 0.0 collective-permute-done.10.refs_4_.refs_3_
  71.4 1.2 collective-permute-start.15
  72.5 2.5 %collective-permute-start.17 = (bf16[16,96,256]{2,1,0:T(8,128)(2,1)}, bf16[16,96,256]{2,1,0:T(8,128)(2,1)S(1)}, u32[]{:S(2)}, u32[]{:S(2)}) collective-permute-start(bf16[16,96,256]{2,1,0:T(8,128)(2,1)} %collective-permute-done.10.refs_4_.refs_3_), channel_id=1, source_target_pairs={{0,3},{1,2},{2,1},{3,0},{4,5},{5,4},{6,7},{7,6},{8,11},{9,10},{10,... | collective-permute-start | bytes 2359304 | tf_op jit(solution)/shard_map/ppermute | solution.py:123
  75.0 2.6 %collective-permute-done.18.refs_8_.refs_7_ = bf16[16,80,256]{2,1,0:T(8,128)(2,1)} collective-permute-done((bf16[16,80,256]{2,1,0:T(8,128)(2,1)S(1)}, bf16[16,80,256]{2,1,0:T(8,128)(2,1)}, u32[]{:S(2)}, u32[]{:S(2)}) %collective-permute-start.18) | collective-permute-done | bytes 655392 | tf_op jit(solution)/shard_map/ppermute | solution.py:123
  77.6 0.7 collective-permute-start.19
  78.2 0.0 collective-permute-done.14.refs_2_.refs_1_
  78.2 0.0 collective-permute-done.16.refs_5_.refs_4_
  78.2 8.4 %shard_map.80.refs_10_ = f32[24,128]{1,0:T(8,128)S(1)} custom-call(s32[66]{0:T(128)S(1)} %pad_add_fusion.place_ref, bf16[16,96,256]{2,1,0:T(8,128)(2,1)S(1)} %pad_maximum_fusion.refs_0_, bf16[16,96,256]{2,1,0:T(8,128)(2,1)S(1)} %collective-permute-done.8.refs_1_.refs_0_, bf16[16,96,256]{2,1,0:T(8,128)(2,1)} %collective-permute-done.14.refs_2_.refs_1_, ...), custom_call_target="tpu_custom_call" | custom-call | flops 7247757312 | bytes 16777216 | tf_op jit(solution)/shard_map/pallas_call | solution.py:280
  86.7 1.4 %collective-permute-done.19.refs_8_ = bf16[16,80,256]{2,1,0:T(8,128)(2,1)S(1)} collective-permute-done((bf16[16,80,256]{2,1,0:T(8,128)(2,1)S(1)}, bf16[16,80,256]{2,1,0:T(8,128)(2,1)S(1)}, u32[]{:S(2)}, u32[]{:S(2)}) %collective-permute-start.19) | collective-permute-done | bytes 655392 | tf_op jit(solution)/shard_map/ppermute | solution.py:123
  88.1 0.0 collective-permute-done.15.refs_2_
  88.1 0.0 collective-permute-done.17.refs_5_
  88.2 12.5 %shard_map.81 = f32[64,128]{1,0:T(8,128)S(1)} custom-call(s32[66]{0:T(128)S(1)} %pad_add_fusion.place_ref, bf16[16,96,256]{2,1,0:T(8,128)(2,1)S(1)} %collective-permute-done.8.refs_1_.refs_0_, bf16[16,96,256]{2,1,0:T(8,128)(2,1)} %collective-permute-done.14.refs_2_.refs_1_, bf16[16,96,256]{2,1,0:T(8,128)(2,1)S(1)} %collective-permute-done.15.refs_2_, ...), custom_call_target="tpu_custom_call" | custom-call | flops 9663676416 | bytes 16777216 | tf_op jit(solution)/shard_map/pallas_call | solution.py:280
  100.6 14.3 %all_to_all.11 = f32[64,1,128]{2,1,0:T(1,128)} all-to-all(f32[64,1,128]{2,1,0:T(1,128)S(1)} %bitcast.6), channel_id=1, replica_groups=mesh['x'=4,'y'=4,'c'=2,'z'=4] {'x','y','z'}, dimensions={0} | all-to-all | bytes 65536 | tf_op jit(solution)/shard_map/all_to_all | solution.py:361
  114.9 1.5 %shard_map.82 = (f32[1,128]{1,0:T(1,128)}, f32[1,100]{1,0:T(1,128)}) custom-call(f32[64,128]{1,0:T(8,128)} %bitcast.7), custom_call_target="tpu_custom_call" | custom-call | tf_op jit(solution)/shard_map/pallas_call | solution.py:317
  (11 shorter events, 0.1 us)
Async XLA Ops:
  2.3 9.1 %collective-permute-start = (bf16[1,272,256]{2,1,0:T(8,128)(2,1)}, bf16[1,272,256]{2,1,0:T(8,128)(2,1)S(1)}, u32[]{:S(2)}, u32[]{:S(2)}) collective-permute-start(bf16[1,272,256]{2,1,0:T(8,128)(2,1)} %shard_map.77), channel_id=1, source_target_pairs={{0,1},{1,0},{2,3},{3,2},{4,7},{5,6},{6,5},{7,4},{8,9},{9,8},{10,11... | collective-permute-start | bytes 417800 | tf_op jit(solution)/shard_map/ppermute | solution.py:123
  4.3 11.2 %collective-permute-start.1 = (bf16[1,272,256]{2,1,0:T(8,128)(2,1)}, bf16[1,272,256]{2,1,0:T(8,128)(2,1)S(1)}, u32[]{:S(2)}, u32[]{:S(2)}) collective-permute-start(bf16[1,272,256]{2,1,0:T(8,128)(2,1)} %shard_map.77), channel_id=1, source_target_pairs={{0,32},{1,33},{2,34},{3,35},{4,100},{5,101},{6,102},{7,103},{8,40}... | collective-permute-start | bytes 417800 | tf_op jit(solution)/shard_map/ppermute | solution.py:123
  5.8 9.8 %collective-permute-start.2 = (bf16[1,272,256]{2,1,0:T(8,128)(2,1)}, bf16[1,272,256]{2,1,0:T(8,128)(2,1)S(1)}, u32[]{:S(2)}, u32[]{:S(2)}) collective-permute-start(bf16[1,272,256]{2,1,0:T(8,128)(2,1)} %shard_map.77), channel_id=1, source_target_pairs={{0,33},{1,32},{2,35},{3,34},{4,103},{5,102},{6,101},{7,100},{8,41}... | collective-permute-start | bytes 417800 | tf_op jit(solution)/shard_map/ppermute | solution.py:123
  5.8 9.8 %collective-permute-start.3 = (bf16[1,272,256]{2,1,0:T(8,128)(2,1)}, bf16[1,272,256]{2,1,0:T(8,128)(2,1)S(1)}, u32[]{:S(2)}, u32[]{:S(2)}) collective-permute-start(bf16[1,272,256]{2,1,0:T(8,128)(2,1)} %shard_map.77), channel_id=1, source_target_pairs={{0,24},{1,25},{2,26},{3,27},{4,12},{5,13},{6,14},{7,15},{8,16},{9,... | collective-permute-start | bytes 417800 | tf_op jit(solution)/shard_map/ppermute | solution.py:123
  8.9 7.4 %collective-permute-start.4 = (bf16[1,272,256]{2,1,0:T(8,128)(2,1)}, bf16[1,272,256]{2,1,0:T(8,128)(2,1)S(1)}, u32[]{:S(2)}, u32[]{:S(2)}) collective-permute-start(bf16[1,272,256]{2,1,0:T(8,128)(2,1)} %shard_map.77), channel_id=1, source_target_pairs={{0,25},{1,24},{2,27},{3,26},{4,15},{5,14},{6,13},{7,12},{8,17},{9,... | collective-permute-start | bytes 417800 | tf_op jit(solution)/shard_map/ppermute | solution.py:123
  11.5 7.5 %collective-permute-start.5 = (bf16[1,272,256]{2,1,0:T(8,128)(2,1)}, bf16[1,272,256]{2,1,0:T(8,128)(2,1)S(1)}, u32[]{:S(2)}, u32[]{:S(2)}) collective-permute-start(bf16[1,272,256]{2,1,0:T(8,128)(2,1)} %shard_map.77), channel_id=1, source_target_pairs={{0,56},{1,57},{2,58},{3,59},{4,108},{5,109},{6,110},{7,111},{8,48}... | collective-permute-start | bytes 417800 | tf_op jit(solution)/shard_map/ppermute | solution.py:123
  15.5 8.4 %collective-permute-start.6 = (bf16[1,272,256]{2,1,0:T(8,128)(2,1)}, bf16[1,272,256]{2,1,0:T(8,128)(2,1)S(1)}, u32[]{:S(2)}, u32[]{:S(2)}) collective-permute-start(bf16[1,272,256]{2,1,0:T(8,128)(2,1)} %shard_map.77), channel_id=1, source_target_pairs={{0,57},{1,56},{2,59},{3,58},{4,111},{5,110},{6,109},{7,108},{8,49}... | collective-permute-start | bytes 417800 | tf_op jit(solution)/shard_map/ppermute | solution.py:123
  16.3 7.7 %copy-start.1 = (bf16[3,3]{1,0:T(4,128)(2,1)S(1)}, bf16[3,3]{1,0:T(4,128)(2,1)}, u32[]{:S(2)}) copy-start(bf16[3,3]{1,0:T(4,128)(2,1)} %tap_q_ref.1) | copy-start | bytes 58
  16.3 7.7 %copy-start.2 = (bf16[3,3]{1,0:T(4,128)(2,1)S(1)}, bf16[3,3]{1,0:T(4,128)(2,1)}, u32[]{:S(2)}) copy-start(bf16[3,3]{1,0:T(4,128)(2,1)} %tap_d_ref.1) | copy-start | bytes 58
  24.0 7.9 %collective-permute-start.7 = (bf16[8,96,256]{2,1,0:T(8,128)(2,1)S(1)}, bf16[8,96,256]{2,1,0:T(8,128)(2,1)S(1)}, u32[]{:S(2)}, u32[]{:S(2)}) collective-permute-start(bf16[8,96,256]{2,1,0:T(8,128)(2,1)S(1)} %get-tuple-element.29), channel_id=1, source_target_pairs={{0,8},{1,9},{2,10},{3,11},{4,28},{5,29},{6,30},{7,31},{8,0},{9,1},... | collective-permute-start | bytes 1179656 | tf_op jit(solution)/shard_map/ppermute | solution.py:123
  24.1 2.2 %copy-start = (bf16[32,256,256]{2,1,0:T(8,128)(2,1)S(1)}, bf16[32,256,256]{2,1,0:T(8,128)(2,1)}, u32[]{:S(2)}) copy-start(bf16[32,256,256]{2,1,0:T(8,128)(2,1)} %maps_hbm) | copy-start | bytes 12582916
  31.9 30.8 %collective-permute-start.13 = (bf16[32,256,256]{2,1,0:T(8,128)(2,1)}, bf16[32,256,256]{2,1,0:T(8,128)(2,1)}, u32[]{:S(2)}, u32[]{:S(2)}) collective-permute-start(bf16[32,256,256]{2,1,0:T(8,128)(2,1)} %get-tuple-element.19.refs_3_), channel_id=1, source_target_pairs={{0,4},{4,0},{1,5},{5,1},{2,6},{6,2},{3,7},{7,3},{8,12},{12,8},{9,1... | collective-permute-start | bytes 12582920 | tf_op jit(solution)/shard_map/ppermute | solution.py:349
  33.8 8.4 %collective-permute-start.11 = (bf16[8,80,256]{2,1,0:T(8,128)(2,1)S(1)}, bf16[8,80,256]{2,1,0:T(8,128)(2,1)S(1)}, u32[]{:S(2)}, u32[]{:S(2)}) collective-permute-start(bf16[8,80,256]{2,1,0:T(8,128)(2,1)S(1)} %slice.11), channel_id=1, source_target_pairs={{0,3},{1,2},{2,1},{3,0},{4,5},{5,4},{6,7},{7,6},{8,11},{9,10},{10,... | collective-permute-start | bytes 983048 | tf_op jit(solution)/shard_map/ppermute | solution.py:123
  42.2 22.1 %copy-start.5 = (s32[8]{0:T(128)S(1)}, s32[8]{0:T(128)}, u32[]{:S(2)}) copy-start(s32[8]{0:T(128)} %constant.41) | copy-start | bytes 100
  42.2 17.4 %collective-permute-start.12 = (bf16[16,80,256]{2,1,0:T(8,128)(2,1)S(1)}, bf16[16,80,256]{2,1,0:T(8,128)(2,1)S(1)}, u32[]{:S(2)}, u32[]{:S(2)}) collective-permute-start(bf16[16,80,256]{2,1,0:T(8,128)(2,1)S(1)} %pad_maximum_fusion.2.refs_2_.refs_6_), channel_id=1, source_target_pairs={{0,96},{1,97},{2,98},{3,99},{4,36},{5,37},{6,38},{7,39},{8,104},{9... | collective-permute-start | bytes 1966088 | tf_op jit(solution)/shard_map/ppermute | solution.py:123
  42.8 15.5 %collective-permute-start.9 = (bf16[8,96,256]{2,1,0:T(8,128)(2,1)S(1)}, bf16[8,96,256]{2,1,0:T(8,128)(2,1)S(1)}, u32[]{:S(2)}, u32[]{:S(2)}) collective-permute-start(bf16[8,96,256]{2,1,0:T(8,128)(2,1)S(1)} %get-tuple-element.28), channel_id=1, source_target_pairs={{0,96},{1,97},{2,98},{3,99},{4,36},{5,37},{6,38},{7,39},{8,104},{9... | collective-permute-start | bytes 1179656 | tf_op jit(solution)/shard_map/ppermute | solution.py:123
  45.5 25.8 %collective-permute-start.8 = (bf16[16,96,256]{2,1,0:T(8,128)(2,1)S(1)}, bf16[16,96,256]{2,1,0:T(8,128)(2,1)S(1)}, u32[]{:S(2)}, u32[]{:S(2)}) collective-permute-start(bf16[16,96,256]{2,1,0:T(8,128)(2,1)S(1)} %pad_maximum_fusion.refs_0_), channel_id=1, source_target_pairs={{0,3},{1,2},{2,1},{3,0},{4,5},{5,4},{6,7},{7,6},{8,11},{9,10},{10,... | collective-permute-start | bytes 2359304 | tf_op jit(solution)/shard_map/ppermute | solution.py:123
  58.4 13.0 %collective-permute-start.10 = (bf16[16,96,256]{2,1,0:T(8,128)(2,1)S(1)}, bf16[16,96,256]{2,1,0:T(8,128)(2,1)}, u32[]{:S(2)}, u32[]{:S(2)}) collective-permute-start(bf16[16,96,256]{2,1,0:T(8,128)(2,1)S(1)} %pad_maximum_fusion.1.refs_1_.refs_3_), channel_id=1, source_target_pairs={{0,8},{1,9},{2,10},{3,11},{4,28},{5,29},{6,30},{7,31},{8,0},{9,1},... | collective-permute-start | bytes 2359304 | tf_op jit(solution)/shard_map/ppermute | solution.py:123
  59.1 19.1 %collective-permute-start.14 = (bf16[16,96,256]{2,1,0:T(8,128)(2,1)S(1)}, bf16[16,96,256]{2,1,0:T(8,128)(2,1)}, u32[]{:S(2)}, u32[]{:S(2)}) collective-permute-start(bf16[16,96,256]{2,1,0:T(8,128)(2,1)S(1)} %pad_maximum_fusion.refs_0_), channel_id=1, source_target_pairs={{0,96},{1,97},{2,98},{3,99},{4,36},{5,37},{6,38},{7,39},{8,104},{9... | collective-permute-start | bytes 2359304 | tf_op jit(solution)/shard_map/ppermute | solution.py:123
  59.6 0.8 copy-start.3
  60.4 17.8 %collective-permute-start.16 = (bf16[16,96,256]{2,1,0:T(8,128)(2,1)S(1)}, bf16[16,96,256]{2,1,0:T(8,128)(2,1)}, u32[]{:S(2)}, u32[]{:S(2)}) collective-permute-start(bf16[16,96,256]{2,1,0:T(8,128)(2,1)S(1)} %pad_maximum_fusion.1.refs_1_.refs_3_), channel_id=1, source_target_pairs={{0,3},{1,2},{2,1},{3,0},{4,5},{5,4},{6,7},{7,6},{8,11},{9,10},{10,... | collective-permute-start | bytes 2359304 | tf_op jit(solution)/shard_map/ppermute | solution.py:123
  62.7 14.8 %collective-permute-start.18 = (bf16[16,80,256]{2,1,0:T(8,128)(2,1)S(1)}, bf16[16,80,256]{2,1,0:T(8,128)(2,1)}, u32[]{:S(2)}, u32[]{:S(2)}) collective-permute-start(bf16[16,80,256]{2,1,0:T(8,128)(2,1)S(1)} %pad_maximum_fusion.2.refs_2_.refs_6_), channel_id=1, source_target_pairs={{0,8},{1,9},{2,10},{3,11},{4,28},{5,29},{6,30},{7,31},{8,0},{9,1},... | collective-permute-start | bytes 1966088 | tf_op jit(solution)/shard_map/ppermute | solution.py:123
  64.5 13.1 %copy-start.4 = (bf16[16,80,256]{2,1,0:T(8,128)(2,1)S(1)}, bf16[16,80,256]{2,1,0:T(8,128)(2,1)}, u32[]{:S(2)}) copy-start(bf16[16,80,256]{2,1,0:T(8,128)(2,1)} %copy-done.3) | copy-start | bytes 1966084
  71.4 16.8 %collective-permute-start.15 = (bf16[16,96,256]{2,1,0:T(8,128)(2,1)S(1)}, bf16[16,96,256]{2,1,0:T(8,128)(2,1)S(1)}, u32[]{:S(2)}, u32[]{:S(2)}) collective-permute-start(bf16[16,96,256]{2,1,0:T(8,128)(2,1)S(1)} %collective-permute-done.8.refs_1_.refs_0_), channel_id=1, source_target_pairs={{0,96},{1,97},{2,98},{3,99},{4,36},{5,37},{6,38},{7,39},{8,104},{9... | collective-permute-start | bytes 2359304 | tf_op jit(solution)/shard_map/ppermute | solution.py:123
  72.5 15.6 %collective-permute-start.17 = (bf16[16,96,256]{2,1,0:T(8,128)(2,1)}, bf16[16,96,256]{2,1,0:T(8,128)(2,1)S(1)}, u32[]{:S(2)}, u32[]{:S(2)}) collective-permute-start(bf16[16,96,256]{2,1,0:T(8,128)(2,1)} %collective-permute-done.10.refs_4_.refs_3_), channel_id=1, source_target_pairs={{0,3},{1,2},{2,1},{3,0},{4,5},{5,4},{6,7},{7,6},{8,11},{9,10},{10,... | collective-permute-start | bytes 2359304 | tf_op jit(solution)/shard_map/ppermute | solution.py:123
  77.6 10.6 %collective-permute-start.19 = (bf16[16,80,256]{2,1,0:T(8,128)(2,1)S(1)}, bf16[16,80,256]{2,1,0:T(8,128)(2,1)S(1)}, u32[]{:S(2)}, u32[]{:S(2)}) collective-permute-start(bf16[16,80,256]{2,1,0:T(8,128)(2,1)S(1)} %copy-done.4), channel_id=1, source_target_pairs={{0,8},{1,9},{2,10},{3,11},{4,28},{5,29},{6,30},{7,31},{8,0},{9,1},... | collective-permute-start | bytes 1966088 | tf_op jit(solution)/shard_map/ppermute | solution.py:123
